TPU v7x, 512 devices: a whole 4x8x8 slice. The times are simulated.
512 devices in a mesh: level: 16 (over z_hi, y), req: 32 (over z_lo, x, core).
Axes of the slice: x: 4, y: 8, z: 8 (z_hi: 2, z_lo: 4; z = z_hi * 4 + z_lo), core: 2. Of those that a mesh axis runs over, the one named last changes fastest.
Arguments:
- queries: bfloat16 [256, 256, 896], P('level', 'req'), may hold values from -120 to 120
- out_grad: bfloat16 [256, 256, 896], P('level', 'req'), may hold values from -5 to 5
- resp_key: bfloat16 [256, 256, 128], P('level', 'req'), may hold values from -4 to 4
- resp_value: bfloat16 [256, 256, 128], P('level', 'req'), may hold values from -4 to 4
- sys_key: bfloat16 [512, 128], P('level'), may hold values from -4 to 4
- sys_value: bfloat16 [512, 128], P('level'), may hold values from -4 to 4
- ctx_key: bfloat16 [64, 512, 128], P('req', 'level'), may hold values from -4 to 4
- ctx_value: bfloat16 [64, 512, 128], P('req', 'level'), may hold values from -4 to 4
- parent: int32 [256], P('req'), may hold values from 0 to 63, as said below
- resp_len: int32 [256], P('req'), may hold values from 64 to 256
- ctx_len: int32 [64], P('req'), may hold values from 128 to 512
Outputs:
- d_queries: float32 [256, 256, 896], P('level', 'req')
- d_sys_key: float32 [512, 128], P(('level', 'req'))
- d_sys_value: float32 [512, 128], P(('level', 'req'))
- d_ctx_key: float32 [64, 512, 128], P('req', 'level')
- d_ctx_value: float32 [64, 512, 128], P('req', 'level')
- d_resp_key: float32 [256, 256, 128], P('level', 'req')
- d_resp_value: float32 [256, 256, 128], P('level', 'req')
Inputs may be any that keep to these rules, and one draw needn't show every extreme that they name: Response i's parent is one of the contexts (i // 8) * 2 to (i // 8 + 1) * 2 - 1.
All inputs are finite; a program needn't handle non-finite values.
Results may differ from a plain program's by a relative error of at most 0.0049.
Values may be sent and summed in bfloat16 or wider, within the bound.
No kernel may reach another device: no remote copies, remote signals or barrier semaphores. Data moves between devices by JAX's collectives and lax.ppermute only.
A program may use at most 64 MiB of HBM per device.

v0:
```python
import jax
import jax.numpy as jnp
from jax import lax
from jax.sharding import PartitionSpec as P

HEADS = 7
HEAD_DIM = 128
CTX_PER = 2


NEGATIVE = -1e30
HIGHEST = lax.Precision.HIGHEST


def stacked(key_rows, block_width):
    count = key_rows.shape[1] // block_width
    return jnp.swapaxes(
        key_rows.reshape(key_rows.shape[0], count, block_width, key_rows.shape[2]), 0, 1
    )


def allowed_mask(block_start, block_width, limits, causal, row_places):
    places = block_start + jnp.arange(block_width, dtype=jnp.int32)
    allowed = places[None, :, None, None] < limits[:, None, None, None]
    if causal:
        allowed = allowed & (places[None, :, None, None] <= row_places[None, None, None, :])
    return allowed


def block_scores(key_block, queries_all):
    return jnp.einsum(
        "rkd,trhd->rkht", key_block, queries_all, preferred_element_type=jnp.float32
    ) * HEAD_DIM ** (-0.5)


def forward_segment(
    partials, key_rows, value_rows, limits, causal, row_places, queries_all, grads_all
):
    block_width = min(128, key_rows.shape[1])
    starts = block_width * jnp.arange(key_rows.shape[1] // block_width, dtype=jnp.int32)

    def forward_advance(carried, pieces):
        key_block, value_block, block_start = pieces
        maxima, totals, running = carried
        allowed = allowed_mask(block_start, block_width, limits, causal, row_places)
        scores = block_scores(key_block, queries_all)
        new_max = jnp.maximum(maxima, jnp.max(jnp.where(allowed, scores, NEGATIVE), axis=1))
        weights = jnp.where(allowed, jnp.exp(scores - new_max[:, None]), 0.0)
        shrink = jnp.exp(maxima - new_max)
        totals = shrink * totals + jnp.sum(weights, axis=1)
        products = jnp.einsum(
            "rkd,trhd->rkht", value_block, grads_all, preferred_element_type=jnp.float32
        )
        running = shrink * running + jnp.sum(weights * products, axis=1)
        return ((new_max, totals, running), None)

    partials, unused = lax.scan(
        forward_advance,
        partials,
        (stacked(key_rows, block_width), stacked(value_rows, block_width), starts),
    )
    return partials


def backward_segment(
    query_sum,
    key_rows,
    value_rows,
    limits,
    causal,
    row_places,
    queries_all,
    grads_all,
    logsum,
    deltas,
    shared,
):
    block_width = min(128, key_rows.shape[1])
    starts = block_width * jnp.arange(key_rows.shape[1] // block_width, dtype=jnp.int32)
    scaling = HEAD_DIM ** (-0.5)
    grad_form = "rkht,trhd->kd" if shared else "rkht,trhd->rkd"

    def backward_advance(carried, pieces):
        key_block, value_block, block_start = pieces
        allowed = allowed_mask(block_start, block_width, limits, causal, row_places)
        scores = block_scores(key_block, queries_all)
        chances = jnp.where(allowed, jnp.exp(scores - logsum[:, None]), 0.0)
        products = jnp.einsum(
            "rkd,trhd->rkht", value_block, grads_all, preferred_element_type=jnp.float32
        )
        slopes = (chances * (products - deltas[:, None])).astype(jnp.bfloat16)
        carried = carried + scaling * jnp.einsum(
            "rkht,rkd->trhd", slopes, key_block, preferred_element_type=jnp.float32
        )
        key_grad = scaling * jnp.einsum(
            grad_form, slopes, queries_all, preferred_element_type=jnp.float32
        )
        value_grad = jnp.einsum(
            grad_form, chances.astype(jnp.bfloat16), grads_all, preferred_element_type=jnp.float32
        )
        return (carried, (key_grad, value_grad))

    query_sum, grads_pair = lax.scan(
        backward_advance,
        query_sum,
        (stacked(key_rows, block_width), stacked(value_rows, block_width), starts),
    )
    if shared:
        key_grads = grads_pair[0].reshape(key_rows.shape[1], key_rows.shape[2])
        value_grads = grads_pair[1].reshape(key_rows.shape[1], key_rows.shape[2])
    else:
        key_grads = jnp.swapaxes(grads_pair[0], 0, 1).reshape(key_rows.shape)
        value_grads = jnp.swapaxes(grads_pair[1], 0, 1).reshape(value_rows.shape)
    return (query_sum, key_grads, value_grads)


def shards(
    queries,
    out_grad,
    resp_key,
    resp_value,
    sys_key,
    sys_value,
    ctx_key,
    ctx_value,
    parent,
    resp_len,
    ctx_len,
):
    sys_keys, sys_values, ctx_keys_all, ctx_values_all, own_keys, own_values = (
        lax.all_gather(sys_key, "level", axis=0, tiled=True),
        lax.all_gather(sys_value, "level", axis=0, tiled=True),
        lax.all_gather(ctx_key, "level", axis=1, tiled=True),
        lax.all_gather(ctx_value, "level", axis=1, tiled=True),
        lax.all_gather(resp_key, "level", axis=0, tiled=True),
        lax.all_gather(resp_value, "level", axis=0, tiled=True),
    )
    length = queries.shape[0]
    responses = queries.shape[1]
    row_places = lax.axis_index("level") * length + jnp.arange(length, dtype=jnp.int32)
    queries_all = queries.reshape(length, responses, HEADS, HEAD_DIM)
    live_rows = row_places[:, None] < resp_len[None, :]
    grads_all = jnp.where(
        live_rows[:, :, None, None],
        out_grad.reshape(length, responses, HEADS, HEAD_DIM),
        jnp.zeros((), jnp.bfloat16),
    )
    local_parent = parent - lax.axis_index("req") * CTX_PER
    choose = local_parent[:, None] == jnp.arange(CTX_PER, dtype=jnp.int32)[None, :]
    choose_low = choose.astype(jnp.bfloat16)
    choose_float = choose.astype(jnp.float32)
    ctx_limits = jnp.sum(jnp.where(choose, ctx_len[None, :], 0), axis=1)
    ctx_keys = jnp.einsum(
        "rc,cnd->rnd", choose_low, ctx_keys_all, preferred_element_type=jnp.float32
    ).astype(jnp.bfloat16)
    ctx_values = jnp.einsum(
        "rc,cnd->rnd", choose_low, ctx_values_all, preferred_element_type=jnp.float32
    ).astype(jnp.bfloat16)
    sys_keys = jnp.broadcast_to(sys_keys[None], (responses,) + sys_keys.shape)
    sys_values = jnp.broadcast_to(sys_values[None], (responses,) + sys_values.shape)
    own_keys = jnp.swapaxes(own_keys, 0, 1)
    own_values = jnp.swapaxes(own_values, 0, 1)
    open_limits = jnp.full((responses,), 2**30, jnp.int32)
    segments = [
        (sys_keys, sys_values, open_limits, False, True),
        (ctx_keys, ctx_values, ctx_limits, False, False),
        (own_keys, own_values, open_limits, True, False),
    ]
    maxima = jnp.full((responses, HEADS, length), NEGATIVE, jnp.float32)
    totals = jnp.zeros((responses, HEADS, length), jnp.float32)
    running = jnp.zeros((responses, HEADS, length), jnp.float32)
    partials = (maxima, totals, running)
    for key_rows, value_rows, limits, causal, shared in segments:
        partials = forward_segment(
            partials, key_rows, value_rows, limits, causal, row_places, queries_all, grads_all
        )
    maxima, totals, running = partials
    deltas = running / totals
    logsum = maxima + jnp.log(totals)
    query_sum = jnp.zeros((length, responses, HEADS, HEAD_DIM), jnp.float32)
    results = []
    for key_rows, value_rows, limits, causal, shared in segments:
        query_sum, key_grads, value_grads = backward_segment(
            query_sum,
            key_rows,
            value_rows,
            limits,
            causal,
            row_places,
            queries_all,
            grads_all,
            logsum,
            deltas,
            shared,
        )
        results.append((key_grads, value_grads))
    sys_kpart, sys_vpart = results[0]
    ctx_kpart = jnp.einsum("rc,rnd->ncd", choose_float, results[1][0], precision=HIGHEST)
    ctx_vpart = jnp.einsum("rc,rnd->ncd", choose_float, results[1][1], precision=HIGHEST)
    own_kpart = jnp.swapaxes(results[2][0], 0, 1)
    own_vpart = jnp.swapaxes(results[2][1], 0, 1)
    ctx_kgrad, ctx_vgrad, own_kgrad, own_vgrad = (
        lax.psum_scatter(ctx_kpart, "level", scatter_dimension=0, tiled=True),
        lax.psum_scatter(ctx_vpart, "level", scatter_dimension=0, tiled=True),
        lax.psum_scatter(own_kpart, "level", scatter_dimension=0, tiled=True),
        lax.psum_scatter(own_vpart, "level", scatter_dimension=0, tiled=True),
    )
    sys_kgrad, sys_vgrad = (
        lax.psum_scatter(sys_kpart, ("level", "req"), scatter_dimension=0, tiled=True),
        lax.psum_scatter(sys_vpart, ("level", "req"), scatter_dimension=0, tiled=True),
    )
    d_ctx_key = jnp.swapaxes(ctx_kgrad, 0, 1)
    d_ctx_value = jnp.swapaxes(ctx_vgrad, 0, 1)
    d_queries = query_sum.reshape(length, responses, HEADS * HEAD_DIM)
    return (d_queries, sys_kgrad, sys_vgrad, d_ctx_key, d_ctx_value, own_kgrad, own_vgrad)


def solution(mesh):
    return jax.shard_map(
        shards,
        mesh=mesh,
        in_specs=(
            P("level", "req", None),
            P("level", "req", None),
            P("level", "req", None),
            P("level", "req", None),
            P("level", None),
            P("level", None),
            P("req", "level", None),
            P("req", "level", None),
            P("req"),
            P("req"),
            P("req"),
        ),
        out_specs=(
            P("level", "req", None),
            P(("level", "req"), None),
            P(("level", "req"), None),
            P("req", "level", None),
            P("req", "level", None),
            P("level", "req", None),
            P("level", "req", None),
        ),
        check_vma=False,
    )
```

profile of v0, /device:TPU:1, one launch (start us, length us, event | category | flops | bytes accessed | tf_op | source)
XLA Modules:
  0.0 1298.3 jit_solution(879653468951303531)
XLA Ops:
  10.1 1.7 copy.94
  11.8 51.8 %all_gather.18 = bf16[512,128]{1,0:T(8,128)(2,1)S(1)} all-gather(bf16[32,128]{1,0:T(8,128)(2,1)S(1)} %copy-done.10), channel_id=1, replica_groups=mesh['level'=16,'req'=32] {'level'}, dimensions={0}, use_global_device_ids=true | all-gather | bytes 139264 | tf_op jit(solution)/shard_map/all_gather | solution.py:131
  63.6 39.3 %all_gather.19 = bf16[512,128]{1,0:T(8,128)(2,1)S(1)} all-gather(bf16[32,128]{1,0:T(8,128)(2,1)S(1)} %copy-done.11), channel_id=1, replica_groups=mesh['level'=16,'req'=32] {'level'}, dimensions={0}, use_global_device_ids=true | all-gather | bytes 139264 | tf_op jit(solution)/shard_map/all_gather | solution.py:132
  104.4 14.1 %while.92 = (s32[]{:T(128)}, f32[8,7,16]{2,1,0:T(8,128)S(1)}, f32[8,7,16]{2,1,0:T(8,128)S(1)}, f32[8,7,16]{2,1,0:T(8,128)S(1)}, s32[4]{0:T(128)S(1)}, /*index=5*...) while((s32[]{:T(128)}, f32[8,7,16]{2,1,0:T(8,128)S(1)}, ...), condition=%wide.region_4.5_spmd.clone, body=%wide.region_0.4_spmd.clone.sunk | while | flops 59873664 | bytes 2425356 | solution.py:57
  106.5 1.3 fusion.250
  110.0 1.3 fusion.250
  113.6 1.3 fusion.250
  117.1 1.3 fusion.250
  118.5 42.0 %all_gather.20 = bf16[2,512,128]{2,0,1:T(2,128)(2,1)S(1)} all-gather(bf16[2,32,128]{2,0,1:T(2,128)(2,1)S(1)} %copy.82), channel_id=1, replica_groups=mesh['level'=16,'req'=32] {'level'}, dimensions={1}, use_global_device_ids=true | all-gather | bytes 278528 | tf_op jit(solution)/shard_map/all_gather | solution.py:133
  160.6 40.7 %all_gather.21 = bf16[2,512,128]{2,0,1:T(2,128)(2,1)S(1)} all-gather(bf16[2,32,128]{2,0,1:T(2,128)(2,1)S(1)} %copy.84), channel_id=1, replica_groups=mesh['level'=16,'req'=32] {'level'}, dimensions={1}, use_global_device_ids=true | all-gather | bytes 278528 | tf_op jit(solution)/shard_map/all_gather | solution.py:134
  202.4 1.9 copy_bitcast_fusion
  204.3 17.7 %while.88 = (s32[]{:T(128)}, f32[8,7,16]{2,1,0:T(8,128)S(1)}, f32[8,7,16]{2,1,0:T(8,128)S(1)}, f32[8,7,16]{2,1,0:T(8,128)S(1)}, s32[4]{0:T(128)S(1)}, /*index=5*...) while((s32[]{:T(128)}, f32[8,7,16]{2,1,0:T(8,128)S(1)}, ...), condition=%wide.region_10.11_spmd, body=%wide.region_6.10_spmd.sunk | while | flops 59870976 | bytes 2430109 | solution.py:57
  205.6 1.3 select_reduce_fusion.7
  207.3 1.3 fusion.210
  210.0 1.3 select_reduce_fusion.7
  211.7 1.3 fusion.210
  214.5 1.3 select_reduce_fusion.7
  216.2 1.3 fusion.210
  218.9 1.3 select_reduce_fusion.7
  220.6 1.3 fusion.210
  222.1 44.7 %all_gather.22 = bf16[256,8,128]{2,0,1:T(8,128)(2,1)S(1)} all-gather(bf16[16,8,128]{2,0,1:T(8,128)(2,1)S(1)} %copy.88), channel_id=1, replica_groups=mesh['level'=16,'req'=32] {'level'}, dimensions={0}, use_global_device_ids=true | all-gather | bytes 557056 | tf_op jit(solution)/shard_map/all_gather | solution.py:135
  266.8 43.3 %all_gather.23 = bf16[256,8,128]{2,0,1:T(8,128)(2,1)S(1)} all-gather(bf16[16,8,128]{2,0,1:T(8,128)(2,1)S(1)} %copy.89), channel_id=1, replica_groups=mesh['level'=16,'req'=32] {'level'}, dimensions={0}, use_global_device_ids=true | all-gather | bytes 557056 | tf_op jit(solution)/shard_map/all_gather | solution.py:136
  310.2 6.4 while.90
  317.4 30.5 %while.93 = (s32[]{:T(128)}, f32[16,8,7,128]{3,0,2,1:T(8,128)S(1)}, f32[4,128,128]{2,1,0:T(8,128)}, f32[4,128,128]{2,1,0:T(8,128)}, bf16[4,8,128,128]{3,2,1,0:T(...) while((s32[]{:T(128)}, f32[16,8,7,128]{3,0,2,1:T(8,128)S(1)}, ...), condition=%wide.region_17.18_spmd.clone, body=%wide.region_16.17_spmd.clone.sunk | while | flops 147964160 | bytes 6719347 | solution.py:103
  318.7 2.0 fusion.261
  320.6 1.3 fusion.262
  322.4 1.8 fusion.264
  326.3 2.0 fusion.261
  330.0 1.8 fusion.264
  334.0 2.0 fusion.261
  337.6 1.8 fusion.264
  341.6 2.0 fusion.261
  345.3 1.8 fusion.264
  348.2 29.5 %while.89 = (s32[]{:T(128)}, f32[16,8,7,128]{3,0,2,1:T(8,128)S(1)}, f32[4,8,128,128]{3,2,0,1:T(8,128)}, f32[4,8,128,128]{3,2,0,1:T(8,128)}, bf16[4,8,128,128]{3,...) while((s32[]{:T(128)}, f32[16,8,7,128]{3,0,2,1:T(8,128)S(1)}, ...), condition=%wide.region_19.20_spmd, body=%wide.region_18.19_spmd.sunk | while | flops 147965056 | bytes 6664877 | solution.py:103
  349.6 1.3 fusion.222
  350.8 1.3 fusion.223
  358.2 1.3 fusion.223
  373.0 1.3 fusion.223
  377.8 4.6 fusion.109
  382.4 4.6 fusion.112
  387.1 10.9 while.91
  398.0 2.8 copy.107
  400.9 2.8 copy.108
  404.6 1.3 dynamic-slice.2
  406.6 244.9 %all-reduce.9.cloned.1.call-done = (f32[512,128]{1,0:T(8,128)}, f32[512,128]{1,0:T(8,128)}) async-done(((f32[512,128]{1,0:T(8,128)}, f32[512,128]{1,0:T(8,128)}), (f32[512,128]{1,0:T(8,128)}, f32[512,128]{1,0:T(8,128)})) %all-reduce.9.cloned.1.call-update) | async-done | bytes 524304
  653.9 186.7 %all-reduce.11.cloned.1.call-done = (f32[512,2,128]{2,1,0:T(2,128)}, f32[512,2,128]{2,1,0:T(2,128)}) async-done(((f32[512,2,128]{2,1,0:T(2,128)}, f32[512,2,128]{2,1,0:T(2,128)}), (f32[512,2,128]{2,1,0:T(2,128)}, f32[512,2,128]{2,1,0:T(2,128)})) %all-reduce.11.cloned.1.call-update) | async-done | bytes 1048592
  843.3 225.9 %reduce-scatter.3.cloned.1.call-done = f32[16,8,128]{2,1,0:T(8,128)} async-done(((f32[256,8,128]{2,1,0:T(8,128)}), f32[16,8,128]{2,1,0:T(8,128)}) %reduce-scatter.3.cloned.1.call-update) | async-done | bytes 65552 | tf_op jit(solution)/shard_map/reduce_scatter | solution.py:205
  1069.2 222.6 %reduce-scatter.5.cloned.1.call-done = f32[16,8,128]{2,1,0:T(8,128)} async-done(((f32[256,8,128]{2,1,0:T(8,128)}), f32[16,8,128]{2,1,0:T(8,128)}) %reduce-scatter.5.cloned.1.call-update) | async-done | bytes 65552 | tf_op jit(solution)/shard_map/reduce_scatter | solution.py:206
  (257 shorter events, 83.2 us)
Async XLA Ops:
  7.2 4.6 copy-start.10
  7.2 56.4 %copy-start.11 = (bf16[32,128]{1,0:T(8,128)(2,1)S(1)}, bf16[32,128]{1,0:T(8,128)(2,1)}, u32[]{:S(2)}) copy-start(bf16[32,128]{1,0:T(8,128)(2,1)} %param.28) | copy-start | bytes 24580
  7.2 644.3 %all-reduce.9.cloned.1.call-start = ((), (), s32[]{:S(2)}) async-start(), calls=%async_computation.4 | async-start | bytes 1048576
  104.4 14.1 %copy-start.8 = (bf16[2,32,128]{2,1,0:T(8,128)(2,1)S(1)}, bf16[2,32,128]{2,1,0:T(8,128)(2,1)}, u32[]{:S(2)}) copy-start(bf16[2,32,128]{2,1,0:T(8,128)(2,1)} %param.29) | copy-start | bytes 49156
  104.4 56.2 %copy-start.9 = (bf16[2,32,128]{2,1,0:T(8,128)(2,1)S(1)}, bf16[2,32,128]{2,1,0:T(8,128)(2,1)}, u32[]{:S(2)}) copy-start(bf16[2,32,128]{2,1,0:T(8,128)(2,1)} %param.30) | copy-start | bytes 49156
  104.4 96.8 %copy-start.12 = (s32[8]{0:T(128)S(1)}, s32[8]{0:T(128)}, u32[]{:S(2)}) copy-start(s32[8]{0:T(128)} %param.31) | copy-start | bytes 100
  118.5 83.8 %copy-start.13 = (s32[2]{0:T(128)S(1)}, s32[2]{0:T(128)}, u32[]{:S(2)}) copy-start(s32[2]{0:T(128)} %param.33) | copy-start | bytes 28
  204.3 17.8 %copy-start.6 = (bf16[16,8,128]{2,1,0:T(8,128)(2,1)S(1)}, bf16[16,8,128]{2,1,0:T(8,128)(2,1)}, u32[]{:S(2)}) copy-start(bf16[16,8,128]{2,1,0:T(8,128)(2,1)} %param.25) | copy-start | bytes 98308
  204.3 62.5 %copy-start.7 = (bf16[16,8,128]{2,1,0:T(8,128)(2,1)S(1)}, bf16[16,8,128]{2,1,0:T(8,128)(2,1)}, u32[]{:S(2)}) copy-start(bf16[16,8,128]{2,1,0:T(8,128)(2,1)} %param.26) | copy-start | bytes 98308
  316.6 0.8 copy-start
  317.4 4.5 copy-start.4
  322.2 2.0 copy-start.14
  322.4 2.7 copy-start.5
  325.1 4.5 copy-start.4
  329.9 2.0 copy-start.14
  330.0 2.7 copy-start.5
  332.7 4.5 copy-start.4
  337.5 2.0 copy-start.14
  337.6 2.7 copy-start.5
  340.3 4.5 copy-start.4
  345.1 2.0 copy-start.14
  345.2 2.7 copy-start.5
  348.0 492.5 %all-reduce.11.cloned.1.call-start = ((), (), s32[]{:S(2)}) async-start(), calls=%async_computation.5 | async-start | bytes 2097152
  382.4 4.7 copy-start.1
  387.0 682.2 %reduce-scatter.3.cloned.1.call-start = ((), (), s32[]{:S(2)}) async-start(), calls=%async_computation.2 | async-start | bytes 1114112 | tf_op jit(solution)/shard_map/reduce_scatter | solution.py:205
  387.1 2.7 copy-start.2
  390.1 1.0 copy-start.3
  392.6 2.6 copy-start.2
  395.5 1.0 copy-start.3
  400.8 891.0 %reduce-scatter.5.cloned.1.call-start = ((), (), s32[]{:S(2)}) async-start(), calls=%async_computation.3 | async-start | bytes 1114112 | tf_op jit(solution)/shard_map/reduce_scatter | solution.py:206
Sparse Core Ops, SparseCore 0:
  348.1 303.3 all-reduce.8
  654.7 185.7 all-reduce.10
  845.6 223.5 reduce-scatter.2
  1074.8 217.0 reduce-scatter.4
where the time goes:
time: 1300 us
  waiting for transfers between devices  880 us (68%)
  blocking collectives  262 us (20%)
  matrix products  82.4 us (6%)
  local copies, waits for them, and re-layouts  34 us (3%)
  other arithmetic  23.7 us (2%)
  between operations  14.7 us (1%)
    unnamed x6, waiting for transfers between devices  432 us
    reduce_scatter x1, waiting for transfers between devices, shards(): lax.psum_scatter(own_kpart, 'level', scatter_dimension=0, tiled=True)  226 us
    reduce_scatter x1, waiting for transfers between devices, shards(): lax.psum_scatter(own_vpart, 'level', scatter_dimension=0, tiled=True)  223 us
    all_gather x1, blocking collectives, shards(): lax.all_gather(sys_key, 'level', axis=0, tiled=True)  51.8 us
    all_gather x1, blocking collectives, shards(): lax.all_gather(resp_key, 'level', axis=0, tiled=True)  44.7 us
    all_gather x1, blocking collectives, shards(): lax.all_gather(resp_value, 'level', axis=0, tiled=True)  43.3 us
    all_gather x1, blocking collectives, shards(): lax.all_gather(ctx_key, 'level', axis=1, tiled=True)  42 us
    all_gather x1, blocking collectives, shards(): lax.all_gather(ctx_value, 'level', axis=1, tiled=True)  40.7 us
  transfers between devices with their start and end apart: 4, of which 4 were waited for; matrix products, arithmetic and copies ran while one was open for 5% of the time, Pallas kernels for 0%

commit v1 on v0

v1 whole, which is shorter than its diff:
```python
import math

import jax
import jax.numpy as jnp
from jax import lax
from jax.experimental import pallas as pl
from jax.experimental.pallas import tpu as pltpu
from jax.sharding import PartitionSpec as P

HEADS = 7
HEAD_DIM = 128
CTX_PER = 2
LEVELS = 16
RESP_DEV = 8
SPAN = 16
SPLIT = LEVELS // RESP_DEV
PART = SPAN // SPLIT
SYS_ROWS = 32
CTX_ROWS = 32
SYS = SYS_ROWS * LEVELS
CTX = CTX_ROWS * LEVELS
CH = SPAN * LEVELS
KEYS = SYS + CTX + CH
QROWS = PART * HEADS
ROWS = QROWS * LEVELS
WIDTH = HEADS * HEAD_DIM
SCALING = HEAD_DIM**-0.5
NEGATIVE = -1e30
BLOCK = 128
MIB = 1 << 20

IN_Q = 0
IN_G = IN_Q + QROWS
IN_OK = IN_G + QROWS
IN_OV = IN_OK + SPAN
IN_SK = IN_OV + SPAN
IN_SV = IN_SK + SYS_ROWS
IN_CK = IN_SV + SYS_ROWS
IN_CV = IN_CK + CTX_ROWS
IN_ROWS = IN_CV + CTX_ROWS

OUT_SK = 0
OUT_SV = OUT_SK + SYS_ROWS
OUT_CK = OUT_SV + SYS_ROWS
OUT_CV = OUT_CK + CTX_ROWS
OUT_OK = OUT_CV + CTX_ROWS
OUT_OV = OUT_OK + SPAN
OUT_Q = OUT_OV + SPAN
OUT_ROWS = OUT_Q + QROWS

f32 = jnp.float32
bf16 = jnp.bfloat16


def dot(a, b, contract_a, contract_b):
    return lax.dot_general(
        a, b, (((contract_a,), (contract_b,)), ((), ())), preferred_element_type=f32
    )


def swap_matrix(rows_inner, columns_inner):
    size = rows_inner * columns_inner
    row = lax.broadcasted_iota(jnp.int32, (size, size), 0)
    column = lax.broadcasted_iota(jnp.int32, (size, size), 1)
    wanted = (row % columns_inner) * rows_inner + row // columns_inner
    return (column == wanted).astype(bf16)


def flat(ref):
    whole = ref[...].astype(f32)
    return whole.reshape(SPAN * RESP_DEV, whole.shape[2]).astype(bf16)


def pack_kernel(
    parent_ref, q_ref, g_ref, rk_ref, rv_ref, sk_ref, sv_ref, ck_ref, cv_ref, send_ref
):
    swap = swap_matrix(RESP_DEV, SPAN)
    queries = dot(swap, flat(q_ref), 1, 0)
    grads = dot(swap, flat(g_ref), 1, 0)
    own_k = dot(swap, flat(rk_ref), 1, 0).astype(bf16)
    own_v = dot(swap, flat(rv_ref), 1, 0).astype(bf16)
    sys_k = sk_ref[...]
    sys_v = sv_ref[...]
    for response in range(RESP_DEV):
        owner = lax.rem(parent_ref[response], CTX_PER)
        ctx_k = ck_ref[owner]
        ctx_v = cv_ref[owner]
        for part in range(SPLIT):
            to = response * SPLIT + part
            first = response * SPAN + part * PART
            pieces = [
                rows[first : first + PART, head * HEAD_DIM : (head + 1) * HEAD_DIM]
                for rows in (queries, grads)
                for head in range(HEADS)
            ]
            send_ref[to, IN_Q:IN_OK, :] = jnp.concatenate(pieces, axis=0).astype(bf16)
            span = slice(response * SPAN, (response + 1) * SPAN)
            send_ref[to, IN_OK:IN_OV, :] = own_k[span]
            send_ref[to, IN_OV:IN_SK, :] = own_v[span]
            send_ref[to, IN_SK:IN_SV, :] = sys_k
            send_ref[to, IN_SV:IN_CK, :] = sys_v
            send_ref[to, IN_CK:IN_CV, :] = ctx_k
            send_ref[to, IN_CV:IN_ROWS, :] = ctx_v


def main_kernel(
    parent_ref,
    resp_len_ref,
    ctx_len_ref,
    places_ref,
    recv_ref,
    send_ref,
    q_f32,
    g_f32,
    q_low,
    g_low,
    k_all,
    v_all,
    chances_all,
    slopes_all,
):
    level = lax.axis_index("level")
    response = lax.div(level, SPLIT)
    part = lax.rem(level, SPLIT)
    live = resp_len_ref[response]
    ctx_live = ctx_len_ref[lax.rem(parent_ref[response], CTX_PER)]

    inner = lax.broadcasted_iota(jnp.int32, (QROWS, HEAD_DIM), 0) % PART
    for source in range(LEVELS):
        both = recv_ref[source, IN_Q:IN_OK, :].astype(f32)
        here = slice(source * QROWS, (source + 1) * QROWS)
        q_f32[here, :] = both[:QROWS]
        place = inner + (source * SPAN + part * PART)
        g_f32[here, :] = jnp.where(place < live, both[QROWS:], 0.0)
        k_all[source * SYS_ROWS : (source + 1) * SYS_ROWS, :] = recv_ref[source, IN_SK:IN_SV, :]
        v_all[source * SYS_ROWS : (source + 1) * SYS_ROWS, :] = recv_ref[source, IN_SV:IN_CK, :]
        start = SYS + source * CTX_ROWS
        k_all[start : start + CTX_ROWS, :] = recv_ref[source, IN_CK:IN_CV, :]
        v_all[start : start + CTX_ROWS, :] = recv_ref[source, IN_CV:IN_ROWS, :]
        start = SYS + CTX + source * SPAN
        k_all[start : start + SPAN, :] = recv_ref[source, IN_OK:IN_OV, :]
        v_all[start : start + SPAN, :] = recv_ref[source, IN_OV:IN_SK, :]
    q_low[...] = q_f32[...].astype(bf16)
    g_low[...] = g_f32[...].astype(bf16)

    rate = SCALING * math.log2(math.e)

    def step(index, unused):
        at = pl.multiple_of(index * BLOCK, BLOCK)
        q_block = q_low[pl.ds(at, BLOCK), :]
        g_block = g_low[pl.ds(at, BLOCK), :]
        places = places_ref[:, pl.ds(at, BLOCK)] + part * PART
        scores = dot(k_all[...], q_block, 1, 1)
        products = dot(v_all[...], g_block, 1, 1)
        ctx_place = lax.broadcasted_iota(jnp.int32, (CTX, BLOCK), 0)
        own_place = lax.broadcasted_iota(jnp.int32, (CH, BLOCK), 0)
        scores = jnp.concatenate(
            [
                scores[:SYS],
                jnp.where(ctx_place < ctx_live, scores[SYS : SYS + CTX], NEGATIVE),
                jnp.where(own_place <= places, scores[SYS + CTX :], NEGATIVE),
            ],
            axis=0,
        )
        top = jnp.max(scores, axis=0, keepdims=True)
        weights = jnp.exp2((scores - top) * rate)
        share = 1.0 / jnp.sum(weights, axis=0, keepdims=True)
        delta = jnp.sum(weights * products, axis=0, keepdims=True) * share
        chances = weights * share
        chances_all[:, pl.ds(at, BLOCK)] = chances.astype(bf16)
        slopes_all[:, pl.ds(at, BLOCK)] = (chances * (products - delta)).astype(bf16)
        return unused

    lax.fori_loop(0, ROWS // BLOCK, step, 0)

    d_key = (dot(slopes_all[...], q_low[...], 1, 0) * SCALING).astype(bf16)
    d_value = dot(chances_all[...], g_low[...], 1, 0).astype(bf16)
    d_query = (dot(k_all[...], slopes_all[...], 0, 0) * SCALING).T
    for to in range(LEVELS):
        for rows, at, low in ((d_key, OUT_SK, 0), (d_value, OUT_SV, 0), (d_key, OUT_CK, SYS), (d_value, OUT_CV, SYS)):
            start = low + to * SYS_ROWS
            send_ref[to, at : at + SYS_ROWS, :] = rows[start : start + SYS_ROWS]
        start = SYS + CTX + to * SPAN
        send_ref[to, OUT_OK:OUT_OV, :] = d_key[start : start + SPAN]
        send_ref[to, OUT_OV:OUT_Q, :] = d_value[start : start + SPAN]
        send_ref[to, OUT_Q:OUT_ROWS, :] = d_query[to * QROWS : (to + 1) * QROWS].astype(bf16)


def finish_kernel(parent_ref, recv_ref, dq_ref, dck_ref, dcv_ref, dok_ref, dov_ref, dsys_ref):
    swap = swap_matrix(SPAN, RESP_DEV)
    rows = []
    for response in range(RESP_DEV):
        for part in range(SPLIT):
            block = recv_ref[response * SPLIT + part, OUT_Q:OUT_ROWS, :].astype(f32)
            rows.append(
                jnp.concatenate(
                    [block[head * PART : (head + 1) * PART] for head in range(HEADS)], axis=1
                )
            )
    whole = jnp.concatenate(rows, axis=0).astype(bf16)
    dq_ref[...] = dot(swap, whole, 1, 0).reshape(SPAN, RESP_DEV, WIDTH)

    twice = jnp.concatenate([swap] * SPLIT, axis=1)
    for low, out_ref in ((OUT_OK, dok_ref), (OUT_OV, dov_ref)):
        stack = jnp.concatenate(
            [
                recv_ref[response * SPLIT + part, low : low + SPAN, :]
                for part in range(SPLIT)
                for response in range(RESP_DEV)
            ],
            axis=0,
        )
        out_ref[...] = dot(twice, stack, 1, 0).reshape(SPAN, RESP_DEV, HEAD_DIM)

    for low, out_ref in ((OUT_CK, dck_ref), (OUT_CV, dcv_ref)):
        out_ref[...] = jnp.zeros_like(out_ref)
        for response in range(RESP_DEV):
            owner = lax.rem(parent_ref[response], CTX_PER)
            block = out_ref[owner]
            for part in range(SPLIT):
                block += recv_ref[response * SPLIT + part, low : low + CTX_ROWS, :].astype(f32)
            out_ref[owner] = block

    total = recv_ref[0, OUT_SK:OUT_CK, :].astype(f32)
    for source in range(1, LEVELS):
        total += recv_ref[source, OUT_SK:OUT_CK, :].astype(f32)
    dsys_ref[...] = jnp.concatenate([total[:SYS_ROWS], total[SYS_ROWS:]], axis=1)


SMEM = pl.BlockSpec(memory_space=pltpu.SMEM)
VMEM = pl.BlockSpec(memory_space=pltpu.VMEM)


def shards(
    queries, out_grad, resp_key, resp_value, sys_key, sys_value, ctx_key, ctx_value, parent, resp_len, ctx_len
):
    send = pl.pallas_call(
        pack_kernel,
        out_shape=jax.ShapeDtypeStruct((LEVELS, IN_ROWS, HEAD_DIM), bf16),
        in_specs=[SMEM] + [VMEM] * 8,
        out_specs=VMEM,
        compiler_params=pltpu.CompilerParams(vmem_limit_bytes=24 * MIB),
        name="pack",
    )(parent, queries, out_grad, resp_key, resp_value, sys_key, sys_value, ctx_key, ctx_value)
    recv = lax.all_to_all(send, "level", 0, 0, tiled=True)

    column = jnp.arange(ROWS, dtype=jnp.int32)
    places = ((column // QROWS) * SPAN + column % PART)[None, :]
    send = pl.pallas_call(
        main_kernel,
        out_shape=jax.ShapeDtypeStruct((LEVELS, OUT_ROWS, HEAD_DIM), bf16),
        in_specs=[SMEM] * 3 + [VMEM] * 2,
        out_specs=VMEM,
        scratch_shapes=[
            pltpu.VMEM((ROWS, HEAD_DIM), f32),
            pltpu.VMEM((ROWS, HEAD_DIM), f32),
            pltpu.VMEM((ROWS, HEAD_DIM), bf16),
            pltpu.VMEM((ROWS, HEAD_DIM), bf16),
            pltpu.VMEM((KEYS, HEAD_DIM), bf16),
            pltpu.VMEM((KEYS, HEAD_DIM), bf16),
            pltpu.VMEM((KEYS, ROWS), bf16),
            pltpu.VMEM((KEYS, ROWS), bf16),
        ],
        compiler_params=pltpu.CompilerParams(vmem_limit_bytes=48 * MIB),
        name="attention",
    )(parent, resp_len, ctx_len, places, recv)
    recv = lax.all_to_all(send, "level", 0, 0, tiled=True)

    d_queries, d_ctx_key, d_ctx_value, d_resp_key, d_resp_value, d_sys = pl.pallas_call(
        finish_kernel,
        out_shape=[
            jax.ShapeDtypeStruct((SPAN, RESP_DEV, WIDTH), f32),
            jax.ShapeDtypeStruct((CTX_PER, CTX_ROWS, HEAD_DIM), f32),
            jax.ShapeDtypeStruct((CTX_PER, CTX_ROWS, HEAD_DIM), f32),
            jax.ShapeDtypeStruct((SPAN, RESP_DEV, HEAD_DIM), f32),
            jax.ShapeDtypeStruct((SPAN, RESP_DEV, HEAD_DIM), f32),
            jax.ShapeDtypeStruct((SYS_ROWS, 2 * HEAD_DIM), f32),
        ],
        in_specs=[SMEM, VMEM],
        out_specs=[VMEM] * 6,
        compiler_params=pltpu.CompilerParams(vmem_limit_bytes=24 * MIB),
        name="finish",
    )(parent, recv)
    d_sys = lax.all_to_all(d_sys[:, None, :], "req", 0, 0, tiled=True)
    d_sys = jnp.sum(d_sys, axis=0)
    return (
        d_queries,
        d_sys[:, :HEAD_DIM],
        d_sys[:, HEAD_DIM:],
        d_ctx_key,
        d_ctx_value,
        d_resp_key,
        d_resp_value,
    )


def solution(mesh):
    return jax.shard_map(
        shards,
        mesh=mesh,
        in_specs=(
            P("level", "req", None),
            P("level", "req", None),
            P("level", "req", None),
            P("level", "req", None),
            P("level", None),
            P("level", None),
            P("req", "level", None),
            P("req", "level", None),
            P("req"),
            P("req"),
            P("req"),
        ),
        out_specs=(
            P("level", "req", None),
            P(("level", "req"), None),
            P(("level", "req"), None),
            P("req", "level", None),
            P("req", "level", None),
            P("level", "req", None),
            P("level", "req", None),
        ),
        check_vma=False,
    )
```

time: 1300 us -> 117 us (0.09)
  waiting for transfers between devices: 880 us -> 31 us
  blocking collectives: 262 us -> 49.6 us
  matrix products: 82.4 us -> 0 us
  local copies, waits for them, and re-layouts: 34 us -> 7.43 us
  other arithmetic: 23.7 us -> 0.07 us
  starting transfers between devices: 0.34 us -> 16.3 us
  between operations: 14.7 us -> 0.68 us
    reduce_scatter x2 -> x0, waiting for transfers between devices: 449 us -> none  [the longest x1 226 us: shards(): lax.psum_scatter(own_kpart, 'level', scatter_dimension=0, tiled=True)]
    unnamed x6 -> x0, waiting for transfers between devices: 432 us -> none
    all_gather x6 -> x0, blocking collectives: 262 us -> none  [the longest x1 51.8 us: shards(): lax.all_gather(sys_key, 'level', axis=0, tiled=True)]
    dot_general x64 -> x0, matrix products: 75.9 us -> none  [the longest x20 21.1 us: block_scores(): jnp.einsum('rkd,trhd->rkht', key_block, queries_all, preferred_element_ty...]
    all_to_all x0 -> x2, blocking collectives: none -> 49.6 us  [the longest x1 33.6 us: shards(): recv = lax.all_to_all(send, 'level', 0, 0, tiled=True)]
    all_to_all x0 -> x1, waiting for transfers between devices: none -> 31 us  [shards(): recv = lax.all_to_all(send, 'level', 0, 0, tiled=True)]
    all_to_all x0 -> x1, starting transfers between devices: none -> 16.3 us  [shards(): recv = lax.all_to_all(send, 'level', 0, 0, tiled=True)]
  transfers between devices with their start and end apart: 4 -> 1, of which waited for: 4 -> 1; matrix products, arithmetic and copies ran while one was open for 5% -> 0% of each run, Pallas kernels for 0% -> 0%
where the time goes in v1:
time: 117 us; the launch traced here: 116 us
  blocking collectives  49.6 us (42%)
  waiting for transfers between devices  31 us (26%)
  starting transfers between devices  16.3 us (14%)
  Pallas kernels  11 us (9%)
  local copies, waits for them, and re-layouts  7.43 us (6%)
    all_to_all x1, blocking collectives, shards(): recv = lax.all_to_all(send, 'level', 0, 0, tiled=True)  33.6 us
    all_to_all x1, waiting for transfers between devices, shards(): recv = lax.all_to_all(send, 'level', 0, 0, tiled=True)  31 us
    all_to_all x1, starting transfers between devices, shards(): recv = lax.all_to_all(send, 'level', 0, 0, tiled=True)  16.3 us
    all_to_all x1, blocking collectives, shards(): d_sys = lax.all_to_all(d_sys[:, None, :], 'req', 0, 0, tiled=True)  16 us
    pallas_call x1, Pallas kernels, shards(): pl.pallas_call(main_kernel, out_shape=jax.ShapeDtypeStruct((LEVELS, OUT_R...  7.61 us
    unnamed x24, local copies, waits for them, and re-layouts  6.88 us
  transfers between devices with their start and end apart: 1, of which 1 were waited for; matrix products, arithmetic and copies ran while one was open for 0% of the time, Pallas kernels for 0%

profile of v1, /device:TPU:1, one launch (start us, length us, event | category | flops | bytes accessed | tf_op | source)
XLA Modules:
  0.0 116.1 jit_solution(924375065867288756)
XLA Ops:
  0.6 0.0 copy-start
  0.6 0.9 copy-done
  1.6 0.0 copy-start.1
  1.6 0.9 copy-done.1
  2.5 0.0 copy-start.2
  2.5 0.8 copy-done.2
  3.3 0.0 copy-start.3
  3.3 0.8 copy-done.3
  4.0 0.0 copy-start.4
  4.0 0.7 copy-done.4
  4.7 0.0 copy-start.5
  4.8 0.7 copy-done.5
  5.5 0.0 copy-start.6
  5.5 0.7 copy-done.6
  6.2 0.0 copy-start.7
  6.2 0.7 copy-done.7
  6.9 0.0 copy-start.8
  6.9 0.7 copy-done.8
  7.5 1.8 %pack.1 = bf16[16,272,128]{2,1,0:T(8,128)(2,1)} custom-call(s32[8]{0:T(128)S(1)} %copy-done.8, bf16[16,8,896]{2,1,0:T(8,128)(2,1)S(1)} %copy-done, bf16[16,8,896]{2,1,0:T(8,128)(2,1)S(1)} %copy-done.1, bf16[16,8,128]{2,1,0:T(8,128)(2,1)S(1)} %copy-done.2, bf16[16,8,128]{2,1,0:T(8,128)(2,1)S(1)} %copy-done.3, bf16[32,128]{1,0:T(8,128)(2,1)S(1)} %copy-done.6, ...), custom_call_target="tpu_custom_call" | custom-call | tf_op jit(solution)/shard_map/pack/pallas_call | solution.py:237
  9.4 0.0 copy-start.9
  9.4 0.0 copy-start.10
  9.4 0.0 copy-start.11
  9.4 16.3 %all-to-all-start = ((bf16[16,272,128]{2,1,0:T(8,128)(2,1)}), bf16[16,272,128]{2,1,0:T(8,128)(2,1)S(1)}, u32[]{:S(2)}, u32[]{:S(2)}) async-start(bf16[16,272,128]{2,1,0:T(8,128)(2,1)} %pack.1), calls=%async_computation | async-start | bytes 2228224 | tf_op jit(solution)/shard_map/all_to_all | solution.py:245
  25.7 31.0 %all-to-all-done.recv_ref = bf16[16,272,128]{2,1,0:T(8,128)(2,1)S(1)} async-done(((bf16[16,272,128]{2,1,0:T(8,128)(2,1)}), bf16[16,272,128]{2,1,0:T(8,128)(2,1)S(1)}, u32[]{:S(2)}, u32[]{:S(2)}) %all-to-all-start) | async-done | bytes 1114144 | tf_op jit(solution)/shard_map/all_to_all | solution.py:245
  56.7 0.0 copy-done.9
  56.7 0.0 copy-done.10
  56.7 0.0 copy-done.11
  56.7 7.6 %attention.1 = bf16[16,216,128]{2,1,0:T(8,128)(2,1)S(1)} custom-call(s32[8]{0:T(128)S(1)} %copy-done.9, s32[8]{0:T(128)S(1)} %copy-done.10, s32[2]{0:T(128)S(1)} %copy-done.11, s32[1,896]{1,0:T(1,128)S(1)} %fusion.places_ref, bf16[16,272,128]{2,1,0:T(8,128)(2,1)S(1)} %all-to-all-done.recv_ref), custom_call_target="tpu_custom_call" | custom-call | tf_op jit(solution)/shard_map/attention/pallas_call | solution.py:249
  64.3 33.6 %all_to_all.15.recv_ref = bf16[16,216,128]{2,1,0:T(8,128)(2,1)S(1)} all-to-all(bf16[16,216,128]{2,1,0:T(8,128)(2,1)S(1)} %attention.1), channel_id=1, replica_groups=mesh['level'=16,'req'=32] {'level'}, dimensions={0} | all-to-all | bytes 1769472 | tf_op jit(solution)/shard_map/all_to_all | solution.py:267
  97.9 1.6 %finish.1 = (f32[16,8,896]{2,1,0:T(8,128)}, f32[2,32,128]{2,1,0:T(8,128)}, f32[2,32,128]{2,1,0:T(8,128)}, f32[16,8,128]{2,1,0:T(8,128)}, f32[16,8,128]{2,1,0:T(8,128)}, /*index=5*/f32[32,256]{1,0:T(8,128)S(1)}) custom-call(s32[8]{0:T(128)S(1)} %copy-done.9, bf16[16,216,128]{2,1,0:T(8,128)(2,1)S(1)} %all_to_all.15.recv_ref), custom_call_target="tpu_custom_call" | custom-call | tf_op jit(solution)/shard_map/finish/pallas_call | solution.py:269
  99.5 16.0 %all_to_all.16 = f32[32,1,256]{2,1,0:T(1,128)S(1)} all-to-all(f32[32,1,256]{2,1,0:T(1,128)S(1)} %copy.18), channel_id=1, replica_groups=mesh['level'=16,'req'=32] {'req'}, dimensions={0} | all-to-all | bytes 65536 | tf_op jit(solution)/shard_map/all_to_all | solution.py:284
  115.5 0.1 reduce_sum.11
  115.5 0.5 fusion.2
  (2 shorter events, 0.1 us)
Async XLA Ops:
  0.6 0.9 copy-start
  1.6 0.9 copy-start.1
  2.5 0.8 copy-start.2
  3.3 0.8 copy-start.3
  4.0 0.7 copy-start.4
  4.7 0.7 copy-start.5
  5.5 0.7 copy-start.6
  6.2 0.7 copy-start.7
  6.9 0.7 copy-start.8
  9.4 47.3 %copy-start.9 = (s32[8]{0:T(128)S(1)}, s32[8]{0:T(128)}, u32[]{:S(2)}) copy-start(s32[8]{0:T(128)} %parent_ref.5) | copy-start | bytes 100
  9.4 47.3 %copy-start.10 = (s32[8]{0:T(128)S(1)}, s32[8]{0:T(128)}, u32[]{:S(2)}) copy-start(s32[8]{0:T(128)} %resp_len_ref.1) | copy-start | bytes 100
  9.4 47.3 %copy-start.11 = (s32[2]{0:T(128)S(1)}, s32[2]{0:T(128)}, u32[]{:S(2)}) copy-start(s32[2]{0:T(128)} %ctx_len_ref.1) | copy-start | bytes 28
  9.4 47.3 %all-to-all-start = ((bf16[16,272,128]{2,1,0:T(8,128)(2,1)}), bf16[16,272,128]{2,1,0:T(8,128)(2,1)S(1)}, u32[]{:S(2)}, u32[]{:S(2)}) async-start(bf16[16,272,128]{2,1,0:T(8,128)(2,1)} %pack.1), calls=%async_computation | async-start | bytes 2228224 | tf_op jit(solution)/shard_map/all_to_all | solution.py:245

commit v2 on v1

v2 whole, which is shorter than its diff:
```python
import math

import jax
import jax.numpy as jnp
from jax import lax
from jax.experimental import pallas as pl
from jax.experimental.pallas import tpu as pltpu
from jax.sharding import PartitionSpec as P

HEADS = 7
HEAD_DIM = 128
CTX_PER = 2
LEVELS = 16
RESP_DEV = 8
SPAN = 16
SPLIT = LEVELS // RESP_DEV
PART = SPAN // SPLIT
SYS_ROWS = 32
CTX_ROWS = 32
SYS = SYS_ROWS * LEVELS
CTX = CTX_ROWS * LEVELS
CH = SPAN * LEVELS
KEYS = SYS + CTX + CH
QROWS = PART * HEADS
ROWS = QROWS * LEVELS
WIDTH = HEADS * HEAD_DIM
SCALING = HEAD_DIM**-0.5
NEGATIVE = -1e30
BLOCK = 256
CHUNK = 64
RATE = SCALING * math.log2(math.e)
MIB = 1 << 20

IN_Q = 0
IN_G = IN_Q + QROWS
IN_OK = IN_G + QROWS
IN_OV = IN_OK + SPAN
IN_SK = IN_OV + SPAN
IN_SV = IN_SK + SYS_ROWS
IN_CK = IN_SV + SYS_ROWS
IN_CV = IN_CK + CTX_ROWS
IN_ROWS = IN_CV + CTX_ROWS

OUT_Q = 0
OUT_S = OUT_Q + QROWS
OUT_CK = OUT_S + 8
OUT_CV = OUT_CK + CTX_ROWS
OUT_OK = OUT_CV + CTX_ROWS
OUT_OV = OUT_OK + SPAN
OUT_ROWS = OUT_OV + SPAN

f32 = jnp.float32
bf16 = jnp.bfloat16


def dot(a, b, contract_a, contract_b):
    return lax.dot_general(
        a, b, (((contract_a,), (contract_b,)), ((), ())), preferred_element_type=f32
    )


def swap_matrix(rows_inner, columns_inner):
    size = rows_inner * columns_inner
    row = lax.broadcasted_iota(jnp.int32, (size, size), 0)
    column = lax.broadcasted_iota(jnp.int32, (size, size), 1)
    wanted = (row % columns_inner) * rows_inner + row // columns_inner
    return (column == wanted).astype(bf16)


def flat(ref):
    whole = ref[...].astype(f32)
    return whole.reshape(SPAN * RESP_DEV, whole.shape[2]).astype(bf16)


def pack_kernel(*refs):
    count = len(PACK_SHAPES)
    given, send_ref, held, sems = refs[:count], refs[count], refs[count + 1 : -1], refs[-1]
    copies = [
        pltpu.make_async_copy(given[i], held[i], sems.at[i]) for i in range(count)
    ]
    for copy in copies:
        copy.start()
    for copy in copies:
        copy.wait()
    q_ref, g_ref, rk_ref, rv_ref, sk_ref, sv_ref, ck_ref, cv_ref, parent_ref = held
    swap = swap_matrix(RESP_DEV, SPAN)
    queries = dot(swap, flat(q_ref), 1, 0)
    grads = dot(swap, flat(g_ref), 1, 0)
    own_k = dot(swap, flat(rk_ref), 1, 0).astype(bf16)
    own_v = dot(swap, flat(rv_ref), 1, 0).astype(bf16)
    sys_k = sk_ref[...]
    sys_v = sv_ref[...]
    for response in range(RESP_DEV):
        owner = lax.rem(parent_ref[response], CTX_PER)
        ctx_k = ck_ref[owner]
        ctx_v = cv_ref[owner]
        for part in range(SPLIT):
            to = response * SPLIT + part
            first = response * SPAN + part * PART
            pieces = [
                rows[first : first + PART, head * HEAD_DIM : (head + 1) * HEAD_DIM]
                for rows in (queries, grads)
                for head in range(HEADS)
            ]
            send_ref[to, IN_Q:IN_OK, :] = jnp.concatenate(pieces, axis=0).astype(bf16)
            span = slice(response * SPAN, (response + 1) * SPAN)
            send_ref[to, IN_OK:IN_OV, :] = own_k[span]
            send_ref[to, IN_OV:IN_SK, :] = own_v[span]
            send_ref[to, IN_SK:IN_SV, :] = sys_k
            send_ref[to, IN_SV:IN_CK, :] = sys_v
            send_ref[to, IN_CK:IN_CV, :] = ctx_k
            send_ref[to, IN_CV:IN_ROWS, :] = ctx_v


def collect(resp_len_ref, recv_ref, q_f32, g_f32, q_low, g_low, k_all, v_all):
    level = lax.axis_index("level")
    response = lax.div(level, SPLIT)
    part = lax.rem(level, SPLIT)
    live = resp_len_ref[response]
    inner = lax.broadcasted_iota(jnp.int32, (QROWS, HEAD_DIM), 0) % PART
    for source in range(LEVELS):
        both = recv_ref[source, IN_Q:IN_OK, :].astype(f32)
        here = slice(source * QROWS, (source + 1) * QROWS)
        q_f32[here, :] = both[:QROWS]
        place = inner + (source * SPAN + part * PART)
        g_f32[here, :] = jnp.where(place < live, both[QROWS:], 0.0)
        k_all[source * SYS_ROWS : (source + 1) * SYS_ROWS, :] = recv_ref[source, IN_SK:IN_SV, :]
        v_all[source * SYS_ROWS : (source + 1) * SYS_ROWS, :] = recv_ref[source, IN_SV:IN_CK, :]
        start = SYS + source * CTX_ROWS
        k_all[start : start + CTX_ROWS, :] = recv_ref[source, IN_CK:IN_CV, :]
        v_all[start : start + CTX_ROWS, :] = recv_ref[source, IN_CV:IN_ROWS, :]
        start = SYS + CTX + source * SPAN
        k_all[start : start + SPAN, :] = recv_ref[source, IN_OK:IN_OV, :]
        v_all[start : start + SPAN, :] = recv_ref[source, IN_OV:IN_SK, :]
    q_low[...] = q_f32[...].astype(bf16)
    g_low[...] = g_f32[...].astype(bf16)
    return response, part


def open_score(scores, first, ctx_live, reach):
    if first < SYS:
        return scores
    if first < SYS + CTX:
        row = lax.broadcasted_iota(jnp.int32, scores.shape, 0)
        return jnp.where(row < ctx_live - (first - SYS), scores, NEGATIVE)
    row = lax.broadcasted_iota(jnp.int32, scores.shape, 0)
    return jnp.where(row + (first - SYS - CTX) <= reach, scores, NEGATIVE)


def eights(rows):
    return rows.reshape(rows.shape[0] // 8, 8, rows.shape[1])


def stats_kernel(
    parent_ref,
    resp_len_ref,
    ctx_len_ref,
    places_ref,
    recv_ref,
    sys_ref,
    logsum_ref,
    delta_ref,
    sys_k,
    sys_v,
    q_f32,
    g_f32,
    q_low,
    g_low,
    k_all,
    v_all,
    scores_all,
    products_all,
    chances_all,
    slopes_all,
):
    response, part = collect(resp_len_ref, recv_ref, q_f32, g_f32, q_low, g_low, k_all, v_all)
    ctx_live = ctx_len_ref[lax.rem(parent_ref[response], CTX_PER)]
    for at in range(0, ROWS, BLOCK):
        width = min(BLOCK, ROWS - at)
        columns = slice(at, at + width)
        scores_all[:, columns] = dot(k_all[...], q_low[columns, :], 1, 1)
        products_all[:, columns] = dot(v_all[...], g_low[columns, :], 1, 1)
        reach = places_ref[:, columns] + part * PART
        top = jnp.full((8, width), NEGATIVE, f32)
        for first in range(0, KEYS, CHUNK):
            rows = slice(first, first + CHUNK)
            scores = open_score(scores_all[rows, columns], first, ctx_live, reach)
            top = jnp.maximum(top, jnp.max(eights(scores), axis=0))
        top = jnp.max(top, axis=0, keepdims=True) * RATE
        total = jnp.zeros((8, width), f32)
        delta = jnp.zeros((8, width), f32)
        for first in range(0, KEYS, CHUNK):
            rows = slice(first, first + CHUNK)
            scores = open_score(scores_all[rows, columns], first, ctx_live, reach)
            weights = jnp.exp2(scores * RATE - top)
            if first < SYS:
                scores_all[rows, columns] = weights
            total += jnp.sum(eights(weights), axis=0)
            delta += jnp.sum(eights(weights * products_all[rows, columns]), axis=0)
        total = jnp.sum(total, axis=0, keepdims=True)
        share = 1.0 / total
        delta = jnp.sum(delta, axis=0, keepdims=True) * share
        logsum_ref[:, columns] = top + jnp.log2(total)
        delta_ref[:, columns] = delta
        for first in range(0, SYS, CHUNK):
            rows = slice(first, first + CHUNK)
            chances = scores_all[rows, columns] * share
            chances_all[rows, columns] = chances.astype(bf16)
            slopes_all[rows, columns] = (chances * (products_all[rows, columns] - delta)).astype(bf16)
    sys_k[...] = dot(slopes_all[...], q_low[...], 1, 0) * SCALING
    sys_v[...] = dot(chances_all[...], g_low[...], 1, 0)
    for to in range(SYS_ROWS):
        rows = [grads[pl.ds(to, LEVELS, stride=SYS_ROWS), :] for grads in (sys_k, sys_v)]
        sys_ref[to] = jnp.concatenate(rows, axis=0).astype(bf16)


def grads_kernel(
    parent_ref,
    resp_len_ref,
    ctx_len_ref,
    places_ref,
    recv_ref,
    logsum_ref,
    delta_ref,
    dk_ref,
    dv_ref,
    dq_ref,
    q_f32,
    g_f32,
    q_low,
    g_low,
    k_all,
    v_all,
    scores_all,
    products_all,
    chances_all,
    slopes_all,
):
    response, part = collect(resp_len_ref, recv_ref, q_f32, g_f32, q_low, g_low, k_all, v_all)
    ctx_live = ctx_len_ref[lax.rem(parent_ref[response], CTX_PER)]
    for at in range(0, ROWS, BLOCK):
        width = min(BLOCK, ROWS - at)
        columns = slice(at, at + width)
        scores_all[:, columns] = dot(k_all[...], q_low[columns, :], 1, 1)
        products_all[:, columns] = dot(v_all[...], g_low[columns, :], 1, 1)
        reach = places_ref[:, columns] + part * PART
        logsum = logsum_ref[:, columns]
        delta = delta_ref[:, columns]
        for first in range(0, KEYS, CHUNK):
            rows = slice(first, first + CHUNK)
            scores = open_score(scores_all[rows, columns], first, ctx_live, reach)
            chances = jnp.exp2(scores * RATE - logsum)
            if first >= SYS:
                chances_all[first - SYS : first - SYS + CHUNK, columns] = chances.astype(bf16)
            slopes_all[rows, columns] = (chances * (products_all[rows, columns] - delta)).astype(bf16)
    dk_ref[...] = (dot(slopes_all[SYS:], q_low[...], 1, 0) * SCALING).astype(bf16)
    dv_ref[...] = dot(chances_all[...], g_low[...], 1, 0).astype(bf16)
    dq_ref[...] = (dot(k_all[...], slopes_all[...], 0, 0) * SCALING).T


def gather_kernel(sys_ref, dk_ref, dv_ref, dq_ref, send_ref):
    total = sys_ref[0].astype(f32)
    for source in range(1, SYS_ROWS):
        total += sys_ref[source].astype(f32)
    high = total.astype(bf16).astype(f32)
    rest = total - high
    row = lax.broadcasted_iota(jnp.int32, (8, HEAD_DIM), 0)
    for to in range(LEVELS):
        sums = jnp.zeros((8, HEAD_DIM), f32)
        for at, piece in enumerate((high[to], rest[to], high[LEVELS + to], rest[LEVELS + to])):
            sums = jnp.where(row == at, piece[None, :], sums)
        rows = dq_ref[to * QROWS : (to + 1) * QROWS, :]
        send_ref[to, OUT_Q:OUT_CK, :] = jnp.concatenate([rows, sums], axis=0).astype(bf16)
        ctx = slice(to * CTX_ROWS, (to + 1) * CTX_ROWS)
        send_ref[to, OUT_CK:OUT_CV, :] = dk_ref[ctx, :]
        send_ref[to, OUT_CV:OUT_OK, :] = dv_ref[ctx, :]
        own = slice(CTX + to * SPAN, CTX + (to + 1) * SPAN)
        send_ref[to, OUT_OK:OUT_OV, :] = dk_ref[own, :]
        send_ref[to, OUT_OV:OUT_ROWS, :] = dv_ref[own, :]


def finish_kernel(parent_ref, recv_ref, dq_ref, dck_ref, dcv_ref, dok_ref, dov_ref, dsk_ref, dsv_ref):
    swap = swap_matrix(SPAN, RESP_DEV)
    rows = []
    sums = jnp.zeros((8, HEAD_DIM), f32)
    for response in range(RESP_DEV):
        for part in range(SPLIT):
            block = recv_ref[response * SPLIT + part, OUT_Q:OUT_CK, :].astype(f32)
            sums = sums + block[QROWS:]
            rows.append(
                jnp.concatenate(
                    [block[head * PART : (head + 1) * PART] for head in range(HEADS)], axis=1
                )
            )
    whole = jnp.concatenate(rows, axis=0).astype(bf16)
    dq_ref[...] = dot(swap, whole, 1, 0).reshape(SPAN, RESP_DEV, WIDTH)

    twice = jnp.concatenate([swap] * SPLIT, axis=1)
    for low, out_ref in ((OUT_OK, dok_ref), (OUT_OV, dov_ref)):
        stack = jnp.concatenate(
            [
                recv_ref[response * SPLIT + part, low : low + SPAN, :]
                for part in range(SPLIT)
                for response in range(RESP_DEV)
            ],
            axis=0,
        )
        out_ref[...] = dot(twice, stack, 1, 0).reshape(SPAN, RESP_DEV, HEAD_DIM)

    for low, out_ref in ((OUT_CK, dck_ref), (OUT_CV, dcv_ref)):
        out_ref[...] = jnp.zeros_like(out_ref)
        for response in range(RESP_DEV):
            owner = lax.rem(parent_ref[response], CTX_PER)
            block = out_ref[owner]
            for part in range(SPLIT):
                block += recv_ref[response * SPLIT + part, low : low + CTX_ROWS, :].astype(f32)
            out_ref[owner] = block

    dsk_ref[...] = sums[0:1] + sums[1:2]
    dsv_ref[...] = sums[2:3] + sums[3:4]


SMEM = pl.BlockSpec(memory_space=pltpu.SMEM)
VMEM = pl.BlockSpec(memory_space=pltpu.VMEM)
HBM = pl.BlockSpec(memory_space=pltpu.HBM)
PACK_SHAPES = (
    [((SPAN, RESP_DEV, WIDTH), bf16)] * 2
    + [((SPAN, RESP_DEV, HEAD_DIM), bf16)] * 2
    + [((SYS_ROWS, HEAD_DIM), bf16)] * 2
    + [((CTX_PER, CTX_ROWS, HEAD_DIM), bf16)] * 2
    + [((RESP_DEV,), jnp.int32)]
)


def shards(
    queries, out_grad, resp_key, resp_value, sys_key, sys_value, ctx_key, ctx_value, parent, resp_len, ctx_len
):
    shape = jax.ShapeDtypeStruct
    send = pl.pallas_call(
        pack_kernel,
        out_shape=shape((LEVELS, IN_ROWS, HEAD_DIM), bf16),
        in_specs=[HBM] * len(PACK_SHAPES),
        out_specs=VMEM,
        scratch_shapes=[pltpu.VMEM(*held) for held in PACK_SHAPES[:-1]]
        + [pltpu.SMEM(*PACK_SHAPES[-1]), pltpu.SemaphoreType.DMA((len(PACK_SHAPES),))],
        compiler_params=pltpu.CompilerParams(vmem_limit_bytes=60 * MIB),
        name="pack",
    )(queries, out_grad, resp_key, resp_value, sys_key, sys_value, ctx_key, ctx_value, parent)
    recv = lax.all_to_all(send, "level", 0, 0, tiled=True)

    column = jnp.arange(ROWS, dtype=jnp.int32)
    places = ((column // QROWS) * SPAN + column % PART)[None, :]
    laid_out = [
        pltpu.VMEM((ROWS, HEAD_DIM), f32),
        pltpu.VMEM((ROWS, HEAD_DIM), f32),
        pltpu.VMEM((ROWS, HEAD_DIM), bf16),
        pltpu.VMEM((ROWS, HEAD_DIM), bf16),
        pltpu.VMEM((KEYS, HEAD_DIM), bf16),
        pltpu.VMEM((KEYS, HEAD_DIM), bf16),
        pltpu.VMEM((KEYS, ROWS), f32),
        pltpu.VMEM((KEYS, ROWS), f32),
    ]
    sys_send, logsum, delta = pl.pallas_call(
        stats_kernel,
        out_shape=[
            shape((SYS_ROWS, 2 * LEVELS, HEAD_DIM), bf16),
            shape((1, ROWS), f32),
            shape((1, ROWS), f32),
        ],
        in_specs=[SMEM] * 3 + [VMEM] * 2,
        out_specs=[VMEM] * 3,
        scratch_shapes=[
            pltpu.VMEM((SYS, HEAD_DIM), f32),
            pltpu.VMEM((SYS, HEAD_DIM), f32),
            *laid_out,
            pltpu.VMEM((SYS, ROWS), bf16),
            pltpu.VMEM((SYS, ROWS), bf16),
        ],
        compiler_params=pltpu.CompilerParams(vmem_limit_bytes=40 * MIB),
        cost_estimate=pl.CostEstimate(
            flops=4 * (KEYS + SYS) * ROWS * HEAD_DIM, bytes_accessed=2 * MIB, transcendentals=KEYS * ROWS
        ),
        name="stats",
    )(parent, resp_len, ctx_len, places, recv)
    sys_recv = lax.all_to_all(sys_send, "req", 0, 0, tiled=True)
    d_key, d_value, d_query = pl.pallas_call(
        grads_kernel,
        out_shape=[
            shape((CTX + CH, HEAD_DIM), bf16),
            shape((CTX + CH, HEAD_DIM), bf16),
            shape((ROWS, HEAD_DIM), f32),
        ],
        in_specs=[SMEM] * 3 + [VMEM] * 4,
        out_specs=[VMEM] * 3,
        scratch_shapes=[
            *laid_out,
            pltpu.VMEM((CTX + CH, ROWS), bf16),
            pltpu.VMEM((KEYS, ROWS), bf16),
        ],
        compiler_params=pltpu.CompilerParams(vmem_limit_bytes=40 * MIB),
        cost_estimate=pl.CostEstimate(
            flops=10 * KEYS * ROWS * HEAD_DIM, bytes_accessed=16 * MIB, transcendentals=KEYS * ROWS
        ),
        name="grads",
    )(parent, resp_len, ctx_len, places, recv, logsum, delta)

    send = pl.pallas_call(
        gather_kernel,
        out_shape=shape((LEVELS, OUT_ROWS, HEAD_DIM), bf16),
        in_specs=[VMEM] * 4,
        out_specs=VMEM,
        compiler_params=pltpu.CompilerParams(vmem_limit_bytes=24 * MIB),
        name="gather",
    )(sys_recv, d_key, d_value, d_query)
    recv = lax.all_to_all(send, "level", 0, 0, tiled=True)

    (
        d_queries,
        d_ctx_key,
        d_ctx_value,
        d_resp_key,
        d_resp_value,
        d_sys_key,
        d_sys_value,
    ) = pl.pallas_call(
        finish_kernel,
        out_shape=[
            shape((SPAN, RESP_DEV, WIDTH), f32),
            shape((CTX_PER, CTX_ROWS, HEAD_DIM), f32),
            shape((CTX_PER, CTX_ROWS, HEAD_DIM), f32),
            shape((SPAN, RESP_DEV, HEAD_DIM), f32),
            shape((SPAN, RESP_DEV, HEAD_DIM), f32),
            shape((1, HEAD_DIM), f32),
            shape((1, HEAD_DIM), f32),
        ],
        in_specs=[SMEM, VMEM],
        out_specs=[VMEM] * 7,
        compiler_params=pltpu.CompilerParams(vmem_limit_bytes=24 * MIB),
        name="finish",
    )(parent, recv)
    return (
        d_queries,
        d_sys_key,
        d_sys_value,
        d_ctx_key,
        d_ctx_value,
        d_resp_key,
        d_resp_value,
    )


def solution(mesh):
    return jax.shard_map(
        shards,
        mesh=mesh,
        in_specs=(
            P("level", "req", None),
            P("level", "req", None),
            P("level", "req", None),
            P("level", "req", None),
            P("level", None),
            P("level", None),
            P("req", "level", None),
            P("req", "level", None),
            P("req"),
            P("req"),
            P("req"),
        ),
        out_specs=(
            P("level", "req", None),
            P(("level", "req"), None),
            P(("level", "req"), None),
            P("req", "level", None),
            P("req", "level", None),
            P("level", "req", None),
            P("level", "req", None),
        ),
        check_vma=False,
    )
```

time: 117 us -> 106 us (0.906)
  blocking collectives: 49.6 us -> 27 us
  starting transfers between devices: 16.3 us -> 25.8 us
  waiting for transfers between devices: 31 us -> 38.8 us
  local copies, waits for them, and re-layouts: 7.43 us -> 0.02 us
  Pallas kernels: 11 us -> 12.3 us
    all_to_all x1 -> x0, blocking collectives: 16 us -> none  [shards(): d_sys = lax.all_to_all(d_sys[:, None, :], 'req', 0, 0, tiled=True)]
    all_to_all x0 -> x1, starting transfers between devices: none -> 9.49 us  [shards(): sys_recv = lax.all_to_all(sys_send, 'req', 0, 0, tiled=True)]
    all_to_all x0 -> x1, waiting for transfers between devices: none -> 7.89 us  [shards(): sys_recv = lax.all_to_all(sys_send, 'req', 0, 0, tiled=True)]
    unnamed x24 -> x6, local copies, waits for them, and re-layouts: 6.88 us -> 0.02 us
    all_to_all x1, blocking collectives: 33.6 us -> 27 us  [shards(): recv = lax.all_to_all(send, 'level', 0, 0, tiled=True)]
    pallas_call x3 -> x5, Pallas kernels: 11 us -> 12.3 us  [the longest x1 5.04 us: shards(): pl.pallas_call(stats_kernel, out_shape=[shape((SYS_ROWS, 2 * LEVELS, HEAD...]
  transfers between devices with their start and end apart: 1 -> 2, of which waited for: 1 -> 2; matrix products, arithmetic and copies ran while one was open for 0% -> 0% of each run, Pallas kernels for 0% -> 3%
where the time goes in v2:
time: 106 us; the launch traced here: 105 us
  waiting for transfers between devices  38.8 us (37%)
  blocking collectives  27 us (25%)
  starting transfers between devices  25.8 us (24%)
  Pallas kernels  12.3 us (12%)
    all_to_all x1, waiting for transfers between devices, shards(): recv = lax.all_to_all(send, 'level', 0, 0, tiled=True)  31 us
    all_to_all x1, blocking collectives, shards(): recv = lax.all_to_all(send, 'level', 0, 0, tiled=True)  27 us
    all_to_all x1, starting transfers between devices, shards(): recv = lax.all_to_all(send, 'level', 0, 0, tiled=True)  16.3 us
    all_to_all x1, starting transfers between devices, shards(): sys_recv = lax.all_to_all(sys_send, 'req', 0, 0, tiled=True)  9.49 us
    all_to_all x1, waiting for transfers between devices, shards(): sys_recv = lax.all_to_all(sys_send, 'req', 0, 0, tiled=True)  7.89 us
    pallas_call x1, Pallas kernels, shards(): pl.pallas_call(stats_kernel, out_shape=[shape((SYS_ROWS, 2 * LEVELS, HEAD...  5.04 us
    pallas_call x1, Pallas kernels, shards(): pl.pallas_call(grads_kernel, out_shape=[shape((CTX + CH, HEAD_DIM), bf16)...  3.22 us
    pallas_call x1, Pallas kernels, shards(): pl.pallas_call(pack_kernel, out_shape=shape((LEVELS, IN_ROWS, HEAD_DIM),...  2.44 us
  transfers between devices with their start and end apart: 2, of which 2 were waited for; matrix products, arithmetic and copies ran while one was open for 0% of the time, Pallas kernels for 3%

profile of v2, /device:TPU:1, one launch (start us, length us, event | category | flops | bytes accessed | tf_op | source)
XLA Modules:
  0.0 104.7 jit_solution(4583652921176692069)
XLA Ops:
  0.6 2.4 %pack.1 = bf16[16,272,128]{2,1,0:T(8,128)(2,1)} custom-call(bf16[16,8,896]{2,1,0:T(8,128)(2,1)} %refs_0_.1, bf16[16,8,896]{2,1,0:T(8,128)(2,1)} %refs_1_.1, bf16[16,8,128]{2,1,0:T(8,128)(2,1)} %refs_2_.1, bf16[16,8,128]{2,1,0:T(8,128)(2,1)} %refs_3_.1, bf16[32,128]{1,0:T(8,128)(2,1)} %refs_4_.1, bf16[32,128]{1,0:T(8,128)(2,1)} %refs_5_.1, ...), custom_call_target="tpu_custom_call" | custom-call | tf_op jit(solution)/shard_map/pack/pallas_call | solution.py:339
  3.1 0.0 copy-start
  3.1 0.0 copy-start.1
  3.1 0.0 copy-start.2
  3.1 16.3 %all-to-all-start = ((bf16[16,272,128]{2,1,0:T(8,128)(2,1)}), bf16[16,272,128]{2,1,0:T(8,128)(2,1)S(1)}, u32[]{:S(2)}, u32[]{:S(2)}) async-start(bf16[16,272,128]{2,1,0:T(8,128)(2,1)} %pack.1), calls=%async_computation | async-start | bytes 2228224 | tf_op jit(solution)/shard_map/all_to_all | solution.py:349
  19.5 31.0 %all-to-all-done.recv_ref = bf16[16,272,128]{2,1,0:T(8,128)(2,1)S(1)} async-done(((bf16[16,272,128]{2,1,0:T(8,128)(2,1)}), bf16[16,272,128]{2,1,0:T(8,128)(2,1)S(1)}, u32[]{:S(2)}, u32[]{:S(2)}) %all-to-all-start) | async-done | bytes 1114144 | tf_op jit(solution)/shard_map/all_to_all | solution.py:349
  50.4 0.0 copy-done
  50.5 0.0 copy-done.1
  50.5 0.0 copy-done.2
  50.5 5.0 %stats.1 = (bf16[32,32,128]{2,1,0:T(8,128)(2,1)}, f32[1,896]{1,0:T(1,128)S(1)}, f32[1,896]{1,0:T(1,128)S(1)}) custom-call(s32[8]{0:T(128)S(1)} %copy-done, s32[8]{0:T(128)S(1)} %copy-done.1, s32[2]{0:T(128)S(1)} %copy-done.2, s32[1,896]{1,0:T(1,128)S(1)} %fusion.places_ref, bf16[16,272,128]{2,1,0:T(8,128)(2,1)S(1)} %all-to-all-done.recv_ref), custom_call_target="tpu_custom_call" | custom-call | flops 822083584 | bytes 2097152 | tf_op jit(solution)/shard_map/stats/pallas_call | solution.py:363
  55.5 9.5 %all-to-all-start.1 = ((bf16[32,32,128]{2,1,0:T(8,128)(2,1)}), bf16[32,32,128]{2,1,0:T(8,128)(2,1)S(1)}, u32[]{:S(2)}, u32[]{:S(2)}) async-start(bf16[32,32,128]{2,1,0:T(8,128)(2,1)} %get-tuple-element.20), calls=%async_computation.1 | async-start | bytes 524288 | tf_op jit(solution)/shard_map/all_to_all | solution.py:385
  65.0 3.2 %grads.1 = (bf16[768,128]{1,0:T(8,128)(2,1)S(1)}, bf16[768,128]{1,0:T(8,128)(2,1)S(1)}, f32[896,128]{1,0:T(8,128)S(1)}) custom-call(s32[8]{0:T(128)S(1)} %copy-done, s32[8]{0:T(128)S(1)} %copy-done.1, s32[2]{0:T(128)S(1)} %copy-done.2, s32[1,896]{1,0:T(1,128)S(1)} %fusion.places_ref, bf16[16,272,128]{2,1,0:T(8,128)(2,1)S(1)} %all-to-all-done.recv_ref, ...), custom_call_target="tpu_custom_call" | custom-call | flops 1468006400 | bytes 16777216 | tf_op jit(solution)/shard_map/grads/pallas_call | solution.py:386
  68.2 7.9 %all-to-all-done.1.sys_ref = bf16[32,32,128]{2,1,0:T(8,128)(2,1)S(1)} async-done(((bf16[32,32,128]{2,1,0:T(8,128)(2,1)}), bf16[32,32,128]{2,1,0:T(8,128)(2,1)S(1)}, u32[]{:S(2)}, u32[]{:S(2)}) %all-to-all-start.1) | async-done | bytes 262176 | tf_op jit(solution)/shard_map/all_to_all | solution.py:385
  76.1 0.1 gather.1
  76.2 27.0 %all_to_all.15.recv_ref = bf16[16,160,128]{2,1,0:T(8,128)(2,1)S(1)} all-to-all(bf16[16,160,128]{2,1,0:T(8,128)(2,1)S(1)} %gather.1), channel_id=1, replica_groups=mesh['level'=16,'req'=32] {'level'}, dimensions={0} | all-to-all | bytes 1310720 | tf_op jit(solution)/shard_map/all_to_all | solution.py:415
  103.2 1.6 %finish.1 = (f32[16,8,896]{2,1,0:T(8,128)}, f32[2,32,128]{2,1,0:T(8,128)}, f32[2,32,128]{2,1,0:T(8,128)}, f32[16,8,128]{2,1,0:T(8,128)}, f32[16,8,128]{2,1,0:T(8...) custom-call(s32[8]{0:T(128)S(1)} %copy-done, bf16[16,160,128]{2,1,0:T(8,128)(2,1)S(1)} %all_to_all.15.recv_ref), custom_call_target="tpu_custom_call" | custom-call | tf_op jit(solution)/shard_map/finish/pallas_call | solution.py:425
  (1 shorter events, 0.0 us)
Async XLA Ops:
  3.1 47.4 %copy-start = (s32[8]{0:T(128)S(1)}, s32[8]{0:T(128)}, u32[]{:S(2)}) copy-start(s32[8]{0:T(128)} %parent_ref.5) | copy-start | bytes 100
  3.1 47.4 %copy-start.1 = (s32[8]{0:T(128)S(1)}, s32[8]{0:T(128)}, u32[]{:S(2)}) copy-start(s32[8]{0:T(128)} %resp_len_ref.3) | copy-start | bytes 100
  3.1 47.4 %copy-start.2 = (s32[2]{0:T(128)S(1)}, s32[2]{0:T(128)}, u32[]{:S(2)}) copy-start(s32[2]{0:T(128)} %ctx_len_ref.3) | copy-start | bytes 28
  3.1 47.3 %all-to-all-start = ((bf16[16,272,128]{2,1,0:T(8,128)(2,1)}), bf16[16,272,128]{2,1,0:T(8,128)(2,1)S(1)}, u32[]{:S(2)}, u32[]{:S(2)}) async-start(bf16[16,272,128]{2,1,0:T(8,128)(2,1)} %pack.1), calls=%async_computation | async-start | bytes 2228224 | tf_op jit(solution)/shard_map/all_to_all | solution.py:349
  55.5 20.6 %all-to-all-start.1 = ((bf16[32,32,128]{2,1,0:T(8,128)(2,1)}), bf16[32,32,128]{2,1,0:T(8,128)(2,1)S(1)}, u32[]{:S(2)}, u32[]{:S(2)}) async-start(bf16[32,32,128]{2,1,0:T(8,128)(2,1)} %get-tuple-element.20), calls=%async_computation.1 | async-start | bytes 524288 | tf_op jit(solution)/shard_map/all_to_all | solution.py:385

commit v3 on v2

--- a/solution.py
+++ b/solution.py
@@ -1,3 +1,4 @@
+import functools
 import math
 
 import jax
@@ -74,7 +75,8 @@
 
 def pack_kernel(*refs):
     count = len(PACK_SHAPES)
-    given, send_ref, held, sems = refs[:count], refs[count], refs[count + 1 : -1], refs[-1]
+    given, out_ref = refs[:count], refs[count]
+    held, send_ref, sems, out_sems = refs[count + 1 : -3], refs[-3], refs[-2], refs[-1]
     copies = [
         pltpu.make_async_copy(given[i], held[i], sems.at[i]) for i in range(count)
     ]
@@ -90,6 +92,7 @@
     own_v = dot(swap, flat(rv_ref), 1, 0).astype(bf16)
     sys_k = sk_ref[...]
     sys_v = sv_ref[...]
+    copies = []
     for response in range(RESP_DEV):
         owner = lax.rem(parent_ref[response], CTX_PER)
         ctx_k = ck_ref[owner]
@@ -110,6 +113,13 @@
             send_ref[to, IN_SV:IN_CK, :] = sys_v
             send_ref[to, IN_CK:IN_CV, :] = ctx_k
             send_ref[to, IN_CV:IN_ROWS, :] = ctx_v
+        both = pl.ds(response * SPLIT, SPLIT)
+        copies.append(
+            pltpu.make_async_copy(send_ref.at[both], out_ref.at[both], out_sems.at[response])
+        )
+        copies[-1].start()
+    for copy in copies:
+        copy.wait()
 
 
 def collect(resp_len_ref, recv_ref, q_f32, g_f32, q_low, g_low, k_all, v_all):
@@ -145,10 +155,6 @@
         return jnp.where(row < ctx_live - (first - SYS), scores, NEGATIVE)
     row = lax.broadcasted_iota(jnp.int32, scores.shape, 0)
     return jnp.where(row + (first - SYS - CTX) <= reach, scores, NEGATIVE)
-
-
-def eights(rows):
-    return rows.reshape(rows.shape[0] // 8, 8, rows.shape[1])
 
 
 def stats_kernel(
@@ -176,35 +182,45 @@
     response, part = collect(resp_len_ref, recv_ref, q_f32, g_f32, q_low, g_low, k_all, v_all)
     ctx_live = ctx_len_ref[lax.rem(parent_ref[response], CTX_PER)]
     for at in range(0, ROWS, BLOCK):
-        width = min(BLOCK, ROWS - at)
-        columns = slice(at, at + width)
+        columns = slice(at, min(at + BLOCK, ROWS))
+        width = columns.stop - at
         scores_all[:, columns] = dot(k_all[...], q_low[columns, :], 1, 1)
         products_all[:, columns] = dot(v_all[...], g_low[columns, :], 1, 1)
-        reach = places_ref[:, columns] + part * PART
+        row = lax.broadcasted_iota(jnp.int32, (8, width), 0)
+        reach = places_ref[:, columns] + part * PART - row
+        left = ctx_live - row
+
+        def open_eight(first):
+            scores = scores_all[first : first + 8, columns]
+            if first < SYS:
+                return scores
+            if first < SYS + CTX:
+                return jnp.where(left > first - SYS, scores, NEGATIVE)
+            return jnp.where(reach >= first - SYS - CTX, scores, NEGATIVE)
+
         top = jnp.full((8, width), NEGATIVE, f32)
-        for first in range(0, KEYS, CHUNK):
-            rows = slice(first, first + CHUNK)
-            scores = open_score(scores_all[rows, columns], first, ctx_live, reach)
-            top = jnp.maximum(top, jnp.max(eights(scores), axis=0))
-        top = jnp.max(top, axis=0, keepdims=True) * RATE
         total = jnp.zeros((8, width), f32)
         delta = jnp.zeros((8, width), f32)
-        for first in range(0, KEYS, CHUNK):
-            rows = slice(first, first + CHUNK)
-            scores = open_score(scores_all[rows, columns], first, ctx_live, reach)
-            weights = jnp.exp2(scores * RATE - top)
-            if first < SYS:
-                scores_all[rows, columns] = weights
-            total += jnp.sum(eights(weights), axis=0)
-            delta += jnp.sum(eights(weights * products_all[rows, columns]), axis=0)
-        total = jnp.sum(total, axis=0, keepdims=True)
-        share = 1.0 / total
-        delta = jnp.sum(delta, axis=0, keepdims=True) * share
-        logsum_ref[:, columns] = top + jnp.log2(total)
+        for start in range(0, KEYS, CHUNK):
+            eights = [open_eight(first) for first in range(start, start + CHUNK, 8)]
+            higher = functools.reduce(jnp.maximum, eights, top)
+            shrink = jnp.exp2((top - higher) * RATE)
+            top, total, delta = higher, total * shrink, delta * shrink
+            for index, scores in enumerate(eights):
+                first = start + index * 8
+                weights = jnp.exp2((scores - top) * RATE)
+                total += weights
+                delta += weights * products_all[first : first + 8, columns]
+        highest = jnp.max(top, axis=0, keepdims=True)
+        shrink = jnp.exp2((top - highest) * RATE)
+        total = jnp.sum(total * shrink, axis=0, keepdims=True)
+        delta = jnp.sum(delta * shrink, axis=0, keepdims=True) / total
+        logsum = highest * RATE + jnp.log2(total)
+        logsum_ref[:, columns] = logsum
         delta_ref[:, columns] = delta
-        for first in range(0, SYS, CHUNK):
-            rows = slice(first, first + CHUNK)
-            chances = scores_all[rows, columns] * share
+        for first in range(0, SYS, 16):
+            rows = slice(first, first + 16)
+            chances = jnp.exp2(scores_all[rows, columns] * RATE - logsum)
             chances_all[rows, columns] = chances.astype(bf16)
             slopes_all[rows, columns] = (chances * (products_all[rows, columns] - delta)).astype(bf16)
     sys_k[...] = dot(slopes_all[...], q_low[...], 1, 0) * SCALING
@@ -279,8 +295,8 @@
         send_ref[to, OUT_OV:OUT_ROWS, :] = dv_ref[own, :]
 
 
-def finish_kernel(parent_ref, recv_ref, dq_ref, dck_ref, dcv_ref, dok_ref, dov_ref, dsk_ref, dsv_ref):
-    swap = swap_matrix(SPAN, RESP_DEV)
+def finish_kernel(parent_ref, swap_ref, recv_ref, dq_ref, dck_ref, dcv_ref, dok_ref, dov_ref, dsk_ref, dsv_ref):
+    swap = swap_ref[...]
     rows = []
     sums = jnp.zeros((8, HEAD_DIM), f32)
     for response in range(RESP_DEV):
@@ -340,9 +356,14 @@
         pack_kernel,
         out_shape=shape((LEVELS, IN_ROWS, HEAD_DIM), bf16),
         in_specs=[HBM] * len(PACK_SHAPES),
-        out_specs=VMEM,
+        out_specs=HBM,
         scratch_shapes=[pltpu.VMEM(*held) for held in PACK_SHAPES[:-1]]
-        + [pltpu.SMEM(*PACK_SHAPES[-1]), pltpu.SemaphoreType.DMA((len(PACK_SHAPES),))],
+        + [
+            pltpu.SMEM(*PACK_SHAPES[-1]),
+            pltpu.VMEM((LEVELS, IN_ROWS, HEAD_DIM), bf16),
+            pltpu.SemaphoreType.DMA((len(PACK_SHAPES),)),
+            pltpu.SemaphoreType.DMA((RESP_DEV,)),
+        ],
         compiler_params=pltpu.CompilerParams(vmem_limit_bytes=60 * MIB),
         name="pack",
     )(queries, out_grad, resp_key, resp_value, sys_key, sys_value, ctx_key, ctx_value, parent)
@@ -433,11 +454,11 @@
             shape((1, HEAD_DIM), f32),
             shape((1, HEAD_DIM), f32),
         ],
-        in_specs=[SMEM, VMEM],
+        in_specs=[SMEM] + [VMEM] * 2,
         out_specs=[VMEM] * 7,
         compiler_params=pltpu.CompilerParams(vmem_limit_bytes=24 * MIB),
         name="finish",
-    )(parent, recv)
+    )(parent, swap_matrix(SPAN, RESP_DEV), recv)
     return (
         d_queries,
         d_sys_key,

time: 106 us -> 106 us (level)
  blocking collectives: 27 us -> 0 us
  waiting for transfers between devices: 38.8 us -> 59.5 us
  starting transfers between devices: 25.8 us -> 31.5 us
    all_to_all x1 -> x0, blocking collectives: 27 us -> none  [shards(): recv = lax.all_to_all(send, 'level', 0, 0, tiled=True)]
    all_to_all x1 -> x2, waiting for transfers between devices: 31 us -> 51.6 us  [shards(): recv = lax.all_to_all(send, 'level', 0, 0, tiled=True)]
    all_to_all x1 -> x2, starting transfers between devices: 16.3 us -> 22 us  [shards(): recv = lax.all_to_all(send, 'level', 0, 0, tiled=True)]
  transfers between devices with their start and end apart: 2 -> 3, of which waited for: 2 -> 3; matrix products, arithmetic and copies ran while one was open for 0% -> 0% of each run, Pallas kernels for 3% -> 3%
where the time goes in v3:
time: 106 us; the launch traced here: 105 us
  waiting for transfers between devices  59.5 us (56%)
  starting transfers between devices  31.5 us (30%)
  Pallas kernels  12.6 us (12%)
    all_to_all x2, waiting for transfers between devices, shards(): recv = lax.all_to_all(send, 'level', 0, 0, tiled=True)  51.6 us
    all_to_all x2, starting transfers between devices, shards(): recv = lax.all_to_all(send, 'level', 0, 0, tiled=True)  22 us
    all_to_all x1, starting transfers between devices, shards(): sys_recv = lax.all_to_all(sys_send, 'req', 0, 0, tiled=True)  9.49 us
    all_to_all x1, waiting for transfers between devices, shards(): sys_recv = lax.all_to_all(sys_send, 'req', 0, 0, tiled=True)  7.89 us
    pallas_call x1, Pallas kernels, shards(): pl.pallas_call(stats_kernel, out_shape=[shape((SYS_ROWS, 2 * LEVELS, HEAD...  4.38 us
    pallas_call x1, Pallas kernels, shards(): pl.pallas_call(grads_kernel, out_shape=[shape((CTX + CH, HEAD_DIM), bf16)...  3.21 us
    pallas_call x1, Pallas kernels, shards(): pl.pallas_call(pack_kernel, out_shape=shape((LEVELS, IN_ROWS, HEAD_DIM),...  2.5 us
  transfers between devices with their start and end apart: 3, of which 3 were waited for; matrix products, arithmetic and copies ran while one was open for 0% of the time, Pallas kernels for 3%

profile of v3, /device:TPU:1, one launch (start us, length us, event | category | flops | bytes accessed | tf_op | source)
XLA Modules:
  0.0 104.5 jit_solution(17978031410054837275)
XLA Ops:
  0.6 2.5 %pack.1 = bf16[16,272,128]{2,1,0:T(8,128)(2,1)} custom-call(bf16[16,8,896]{2,1,0:T(8,128)(2,1)} %refs_0_.1, bf16[16,8,896]{2,1,0:T(8,128)(2,1)} %refs_1_.1, bf16[16,8,128]{2,1,0:T(8,128)(2,1)} %refs_2_.1, bf16[16,8,128]{2,1,0:T(8,128)(2,1)} %refs_3_.1, bf16[32,128]{1,0:T(8,128)(2,1)} %refs_4_.1, bf16[32,128]{1,0:T(8,128)(2,1)} %refs_5_.1, ...), custom_call_target="tpu_custom_call" | custom-call | tf_op jit(solution)/shard_map/pack/pallas_call | solution.py:355
  3.1 0.0 copy-start
  3.2 0.0 copy-start.1
  3.2 0.0 copy-start.2
  3.2 16.3 %all-to-all-start = ((bf16[16,272,128]{2,1,0:T(8,128)(2,1)}), bf16[16,272,128]{2,1,0:T(8,128)(2,1)S(1)}, u32[]{:S(2)}, u32[]{:S(2)}) async-start(bf16[16,272,128]{2,1,0:T(8,128)(2,1)} %pack.1), calls=%async_computation | async-start | bytes 2228224 | tf_op jit(solution)/shard_map/all_to_all | solution.py:370
  19.5 31.0 %all-to-all-done.recv_ref = bf16[16,272,128]{2,1,0:T(8,128)(2,1)S(1)} async-done(((bf16[16,272,128]{2,1,0:T(8,128)(2,1)}), bf16[16,272,128]{2,1,0:T(8,128)(2,1)S(1)}, u32[]{:S(2)}, u32[]{:S(2)}) %all-to-all-start) | async-done | bytes 1114144 | tf_op jit(solution)/shard_map/all_to_all | solution.py:370
  50.5 0.0 copy-done
  50.5 0.0 copy-done.1
  50.5 0.0 copy-done.2
  50.5 4.4 %stats.1 = (bf16[32,32,128]{2,1,0:T(8,128)(2,1)}, f32[1,896]{1,0:T(1,128)S(1)}, f32[1,896]{1,0:T(1,128)S(1)}) custom-call(s32[8]{0:T(128)S(1)} %copy-done, s32[8]{0:T(128)S(1)} %copy-done.1, s32[2]{0:T(128)S(1)} %copy-done.2, s32[1,896]{1,0:T(1,128)S(1)} %fusion.1.places_ref, bf16[16,272,128]{2,1,0:T(8,128)(2,1)S(1)} %all-to-all-done.recv_ref), custom_call_target="tpu_custom_call" | custom-call | flops 822083584 | bytes 2097152 | tf_op jit(solution)/shard_map/stats/pallas_call | solution.py:384
  54.9 9.5 %all-to-all-start.1 = ((bf16[32,32,128]{2,1,0:T(8,128)(2,1)}), bf16[32,32,128]{2,1,0:T(8,128)(2,1)S(1)}, u32[]{:S(2)}, u32[]{:S(2)}) async-start(bf16[32,32,128]{2,1,0:T(8,128)(2,1)} %get-tuple-element.20), calls=%async_computation.1 | async-start | bytes 524288 | tf_op jit(solution)/shard_map/all_to_all | solution.py:406
  64.4 3.2 %grads.1 = (bf16[768,128]{1,0:T(8,128)(2,1)S(1)}, bf16[768,128]{1,0:T(8,128)(2,1)S(1)}, f32[896,128]{1,0:T(8,128)S(1)}) custom-call(s32[8]{0:T(128)S(1)} %copy-done, s32[8]{0:T(128)S(1)} %copy-done.1, s32[2]{0:T(128)S(1)} %copy-done.2, s32[1,896]{1,0:T(1,128)S(1)} %fusion.1.places_ref, bf16[16,272,128]{2,1,0:T(8,128)(2,1)S(1)} %all-to-all-done.recv_ref, ...), custom_call_target="tpu_custom_call" | custom-call | flops 1468006400 | bytes 16777216 | tf_op jit(solution)/shard_map/grads/pallas_call | solution.py:407
  67.6 7.9 %all-to-all-done.1.sys_ref = bf16[32,32,128]{2,1,0:T(8,128)(2,1)S(1)} async-done(((bf16[32,32,128]{2,1,0:T(8,128)(2,1)}), bf16[32,32,128]{2,1,0:T(8,128)(2,1)S(1)}, u32[]{:S(2)}, u32[]{:S(2)}) %all-to-all-start.1) | async-done | bytes 262176 | tf_op jit(solution)/shard_map/all_to_all | solution.py:406
  75.5 0.9 gather.1
  76.4 5.7 %all-to-all-start.2 = ((bf16[16,160,128]{2,1,0:T(8,128)(2,1)}), bf16[16,160,128]{2,1,0:T(8,128)(2,1)S(1)}, u32[]{:S(2)}, u32[]{:S(2)}) async-start(bf16[16,160,128]{2,1,0:T(8,128)(2,1)} %gather.1), calls=%async_computation.2 | async-start | bytes 1310720 | tf_op jit(solution)/shard_map/all_to_all | solution.py:436
  82.1 0.2 fusion.swap_ref
  82.3 20.7 %all-to-all-done.2.recv_ref = bf16[16,160,128]{2,1,0:T(8,128)(2,1)S(1)} async-done(((bf16[16,160,128]{2,1,0:T(8,128)(2,1)}), bf16[16,160,128]{2,1,0:T(8,128)(2,1)S(1)}, u32[]{:S(2)}, u32[]{:S(2)}) %all-to-all-start.2) | async-done | bytes 655392 | tf_op jit(solution)/shard_map/all_to_all | solution.py:436
  103.0 1.6 %finish.1 = (f32[16,8,896]{2,1,0:T(8,128)}, f32[2,32,128]{2,1,0:T(8,128)}, f32[2,32,128]{2,1,0:T(8,128)}, f32[16,8,128]{2,1,0:T(8,128)}, f32[16,8,128]{2,1,0:T(8...) custom-call(s32[8]{0:T(128)S(1)} %copy-done, bf16[128,128]{1,0:T(8,128)(2,1)S(1)} %fusion.swap_ref, ...), custom_call_target="tpu_custom_call" | custom-call | tf_op jit(solution)/shard_map/finish/pallas_call | solution.py:446
  (4 shorter events, 0.0 us)
Async XLA Ops:
  3.1 47.4 %copy-start = (s32[8]{0:T(128)S(1)}, s32[8]{0:T(128)}, u32[]{:S(2)}) copy-start(s32[8]{0:T(128)} %parent_ref.5) | copy-start | bytes 100
  3.2 47.4 %copy-start.1 = (s32[8]{0:T(128)S(1)}, s32[8]{0:T(128)}, u32[]{:S(2)}) copy-start(s32[8]{0:T(128)} %resp_len_ref.3) | copy-start | bytes 100
  3.2 47.3 %copy-start.2 = (s32[2]{0:T(128)S(1)}, s32[2]{0:T(128)}, u32[]{:S(2)}) copy-start(s32[2]{0:T(128)} %ctx_len_ref.3) | copy-start | bytes 28
  3.2 47.3 %all-to-all-start = ((bf16[16,272,128]{2,1,0:T(8,128)(2,1)}), bf16[16,272,128]{2,1,0:T(8,128)(2,1)S(1)}, u32[]{:S(2)}, u32[]{:S(2)}) async-start(bf16[16,272,128]{2,1,0:T(8,128)(2,1)} %pack.1), calls=%async_computation | async-start | bytes 2228224 | tf_op jit(solution)/shard_map/all_to_all | solution.py:370
  54.9 20.6 %all-to-all-start.1 = ((bf16[32,32,128]{2,1,0:T(8,128)(2,1)}), bf16[32,32,128]{2,1,0:T(8,128)(2,1)S(1)}, u32[]{:S(2)}, u32[]{:S(2)}) async-start(bf16[32,32,128]{2,1,0:T(8,128)(2,1)} %get-tuple-element.20), calls=%async_computation.1 | async-start | bytes 524288 | tf_op jit(solution)/shard_map/all_to_all | solution.py:406
  76.4 26.6 %all-to-all-start.2 = ((bf16[16,160,128]{2,1,0:T(8,128)(2,1)}), bf16[16,160,128]{2,1,0:T(8,128)(2,1)S(1)}, u32[]{:S(2)}, u32[]{:S(2)}) async-start(bf16[16,160,128]{2,1,0:T(8,128)(2,1)} %gather.1), calls=%async_computation.2 | async-start | bytes 1310720 | tf_op jit(solution)/shard_map/all_to_all | solution.py:436

commit v4 on v3

--- a/solution.py
+++ b/solution.py
@@ -27,6 +27,9 @@
 WIDTH = HEADS * HEAD_DIM
 SCALING = HEAD_DIM**-0.5
 NEGATIVE = -1e30
+FIRST_IN = 8
+FIRST_SYS = 21
+FIRST_OUT = 8
 BLOCK = 256
 CHUNK = 64
 RATE = SCALING * math.log2(math.e)
@@ -52,6 +55,14 @@
 
 f32 = jnp.float32
 bf16 = jnp.bfloat16
+
+
+def order(first, count):
+    return [(first + place) % count for place in range(count)]
+
+
+def slot(level, first):
+    return (level - first) % LEVELS
 
 
 def dot(a, b, contract_a, contract_b):
@@ -105,15 +116,15 @@
                 for rows in (queries, grads)
                 for head in range(HEADS)
             ]
-            send_ref[to, IN_Q:IN_OK, :] = jnp.concatenate(pieces, axis=0).astype(bf16)
+            send_ref[slot(to, FIRST_IN), IN_Q:IN_OK, :] = jnp.concatenate(pieces, axis=0).astype(bf16)
             span = slice(response * SPAN, (response + 1) * SPAN)
-            send_ref[to, IN_OK:IN_OV, :] = own_k[span]
-            send_ref[to, IN_OV:IN_SK, :] = own_v[span]
-            send_ref[to, IN_SK:IN_SV, :] = sys_k
-            send_ref[to, IN_SV:IN_CK, :] = sys_v
-            send_ref[to, IN_CK:IN_CV, :] = ctx_k
-            send_ref[to, IN_CV:IN_ROWS, :] = ctx_v
-        both = pl.ds(response * SPLIT, SPLIT)
+            send_ref[slot(to, FIRST_IN), IN_OK:IN_OV, :] = own_k[span]
+            send_ref[slot(to, FIRST_IN), IN_OV:IN_SK, :] = own_v[span]
+            send_ref[slot(to, FIRST_IN), IN_SK:IN_SV, :] = sys_k
+            send_ref[slot(to, FIRST_IN), IN_SV:IN_CK, :] = sys_v
+            send_ref[slot(to, FIRST_IN), IN_CK:IN_CV, :] = ctx_k
+            send_ref[slot(to, FIRST_IN), IN_CV:IN_ROWS, :] = ctx_v
+        both = pl.ds(slot(response * SPLIT, FIRST_IN), SPLIT)
         copies.append(
             pltpu.make_async_copy(send_ref.at[both], out_ref.at[both], out_sems.at[response])
         )
@@ -129,19 +140,19 @@
     live = resp_len_ref[response]
     inner = lax.broadcasted_iota(jnp.int32, (QROWS, HEAD_DIM), 0) % PART
     for source in range(LEVELS):
-        both = recv_ref[source, IN_Q:IN_OK, :].astype(f32)
+        both = recv_ref[slot(source, FIRST_IN), IN_Q:IN_OK, :].astype(f32)
         here = slice(source * QROWS, (source + 1) * QROWS)
         q_f32[here, :] = both[:QROWS]
         place = inner + (source * SPAN + part * PART)
         g_f32[here, :] = jnp.where(place < live, both[QROWS:], 0.0)
-        k_all[source * SYS_ROWS : (source + 1) * SYS_ROWS, :] = recv_ref[source, IN_SK:IN_SV, :]
-        v_all[source * SYS_ROWS : (source + 1) * SYS_ROWS, :] = recv_ref[source, IN_SV:IN_CK, :]
+        k_all[source * SYS_ROWS : (source + 1) * SYS_ROWS, :] = recv_ref[slot(source, FIRST_IN), IN_SK:IN_SV, :]
+        v_all[source * SYS_ROWS : (source + 1) * SYS_ROWS, :] = recv_ref[slot(source, FIRST_IN), IN_SV:IN_CK, :]
         start = SYS + source * CTX_ROWS
-        k_all[start : start + CTX_ROWS, :] = recv_ref[source, IN_CK:IN_CV, :]
-        v_all[start : start + CTX_ROWS, :] = recv_ref[source, IN_CV:IN_ROWS, :]
+        k_all[start : start + CTX_ROWS, :] = recv_ref[slot(source, FIRST_IN), IN_CK:IN_CV, :]
+        v_all[start : start + CTX_ROWS, :] = recv_ref[slot(source, FIRST_IN), IN_CV:IN_ROWS, :]
         start = SYS + CTX + source * SPAN
-        k_all[start : start + SPAN, :] = recv_ref[source, IN_OK:IN_OV, :]
-        v_all[start : start + SPAN, :] = recv_ref[source, IN_OV:IN_SK, :]
+        k_all[start : start + SPAN, :] = recv_ref[slot(source, FIRST_IN), IN_OK:IN_OV, :]
+        v_all[start : start + SPAN, :] = recv_ref[slot(source, FIRST_IN), IN_OV:IN_SK, :]
     q_low[...] = q_f32[...].astype(bf16)
     g_low[...] = g_f32[...].astype(bf16)
     return response, part
@@ -227,7 +238,7 @@
     sys_v[...] = dot(chances_all[...], g_low[...], 1, 0)
     for to in range(SYS_ROWS):
         rows = [grads[pl.ds(to, LEVELS, stride=SYS_ROWS), :] for grads in (sys_k, sys_v)]
-        sys_ref[to] = jnp.concatenate(rows, axis=0).astype(bf16)
+        sys_ref[(to - FIRST_SYS) % SYS_ROWS] = jnp.concatenate(rows, axis=0).astype(bf16)
 
 
 def grads_kernel(
@@ -286,13 +297,13 @@
         for at, piece in enumerate((high[to], rest[to], high[LEVELS + to], rest[LEVELS + to])):
             sums = jnp.where(row == at, piece[None, :], sums)
         rows = dq_ref[to * QROWS : (to + 1) * QROWS, :]
-        send_ref[to, OUT_Q:OUT_CK, :] = jnp.concatenate([rows, sums], axis=0).astype(bf16)
+        send_ref[slot(to, FIRST_OUT), OUT_Q:OUT_CK, :] = jnp.concatenate([rows, sums], axis=0).astype(bf16)
         ctx = slice(to * CTX_ROWS, (to + 1) * CTX_ROWS)
-        send_ref[to, OUT_CK:OUT_CV, :] = dk_ref[ctx, :]
-        send_ref[to, OUT_CV:OUT_OK, :] = dv_ref[ctx, :]
+        send_ref[slot(to, FIRST_OUT), OUT_CK:OUT_CV, :] = dk_ref[ctx, :]
+        send_ref[slot(to, FIRST_OUT), OUT_CV:OUT_OK, :] = dv_ref[ctx, :]
         own = slice(CTX + to * SPAN, CTX + (to + 1) * SPAN)
-        send_ref[to, OUT_OK:OUT_OV, :] = dk_ref[own, :]
-        send_ref[to, OUT_OV:OUT_ROWS, :] = dv_ref[own, :]
+        send_ref[slot(to, FIRST_OUT), OUT_OK:OUT_OV, :] = dk_ref[own, :]
+        send_ref[slot(to, FIRST_OUT), OUT_OV:OUT_ROWS, :] = dv_ref[own, :]
 
 
 def finish_kernel(parent_ref, swap_ref, recv_ref, dq_ref, dck_ref, dcv_ref, dok_ref, dov_ref, dsk_ref, dsv_ref):
@@ -301,7 +312,7 @@
     sums = jnp.zeros((8, HEAD_DIM), f32)
     for response in range(RESP_DEV):
         for part in range(SPLIT):
-            block = recv_ref[response * SPLIT + part, OUT_Q:OUT_CK, :].astype(f32)
+            block = recv_ref[slot(response * SPLIT + part, FIRST_OUT), OUT_Q:OUT_CK, :].astype(f32)
             sums = sums + block[QROWS:]
             rows.append(
                 jnp.concatenate(
@@ -315,7 +326,7 @@
     for low, out_ref in ((OUT_OK, dok_ref), (OUT_OV, dov_ref)):
         stack = jnp.concatenate(
             [
-                recv_ref[response * SPLIT + part, low : low + SPAN, :]
+                recv_ref[slot(response * SPLIT + part, FIRST_OUT), low : low + SPAN, :]
                 for part in range(SPLIT)
                 for response in range(RESP_DEV)
             ],
@@ -329,7 +340,7 @@
             owner = lax.rem(parent_ref[response], CTX_PER)
             block = out_ref[owner]
             for part in range(SPLIT):
-                block += recv_ref[response * SPLIT + part, low : low + CTX_ROWS, :].astype(f32)
+                block += recv_ref[slot(response * SPLIT + part, FIRST_OUT), low : low + CTX_ROWS, :].astype(f32)
             out_ref[owner] = block
 
     dsk_ref[...] = sums[0:1] + sums[1:2]
@@ -367,7 +378,7 @@
         compiler_params=pltpu.CompilerParams(vmem_limit_bytes=60 * MIB),
         name="pack",
     )(queries, out_grad, resp_key, resp_value, sys_key, sys_value, ctx_key, ctx_value, parent)
-    recv = lax.all_to_all(send, "level", 0, 0, tiled=True)
+    recv = lax.all_to_all(send, "level", 0, 0, axis_index_groups=[order(FIRST_IN, LEVELS)], tiled=True)
 
     column = jnp.arange(ROWS, dtype=jnp.int32)
     places = ((column // QROWS) * SPAN + column % PART)[None, :]
@@ -403,7 +414,9 @@
         ),
         name="stats",
     )(parent, resp_len, ctx_len, places, recv)
-    sys_recv = lax.all_to_all(sys_send, "req", 0, 0, tiled=True)
+    sys_recv = lax.all_to_all(
+        sys_send, "req", 0, 0, axis_index_groups=[order(FIRST_SYS, SYS_ROWS)], tiled=True
+    )
     d_key, d_value, d_query = pl.pallas_call(
         grads_kernel,
         out_shape=[
@@ -433,7 +446,9 @@
         compiler_params=pltpu.CompilerParams(vmem_limit_bytes=24 * MIB),
         name="gather",
     )(sys_recv, d_key, d_value, d_query)
-    recv = lax.all_to_all(send, "level", 0, 0, tiled=True)
+    recv = lax.all_to_all(
+        send, "level", 0, 0, axis_index_groups=[order(FIRST_OUT, LEVELS)], tiled=True
+    )
 
     (
         d_queries,

time: 106 us -> 99.3 us (0.937)
  the two profiles are of different devices: /device:TPU:1 before, /device:TPU:8 now
where the time goes in v4:
time: 99.3 us; the launch traced here: 99 us
  waiting for transfers between devices  48.6 us (49%)
  starting transfers between devices  36.8 us (37%)
  Pallas kernels  12.6 us (13%)
    all_to_all x1, waiting for transfers between devices, shards(): lax.all_to_all(send, 'level', 0, 0, axis_index_groups=[order(FIRST_IN, LE...  27.1 us
    all_to_all x1, waiting for transfers between devices, shards(): lax.all_to_all(send, 'level', 0, 0, axis_index_groups=[order(FIRST_OUT, L...  17.4 us
    all_to_all x1, starting transfers between devices, shards(): lax.all_to_all(send, 'level', 0, 0, axis_index_groups=[order(FIRST_IN, LE...  16.2 us
    all_to_all x1, starting transfers between devices, shards(): lax.all_to_all(send, 'level', 0, 0, axis_index_groups=[order(FIRST_OUT, L...  11.3 us
    all_to_all x1, starting transfers between devices, shards(): lax.all_to_all(sys_send, 'req', 0, 0, axis_index_groups=[order(FIRST_SYS,...  9.36 us
    pallas_call x1, Pallas kernels, shards(): pl.pallas_call(stats_kernel, out_shape=[shape((SYS_ROWS, 2 * LEVELS, HEAD...  4.38 us
    all_to_all x1, waiting for transfers between devices, shards(): lax.all_to_all(sys_send, 'req', 0, 0, axis_index_groups=[order(FIRST_SYS,...  4.12 us
    pallas_call x1, Pallas kernels, shards(): pl.pallas_call(grads_kernel, out_shape=[shape((CTX + CH, HEAD_DIM), bf16)...  3.21 us
  transfers between devices with their start and end apart: 3, of which 3 were waited for; matrix products, arithmetic and copies ran while one was open for 0% of the time, Pallas kernels for 3%

profile of v4, /device:TPU:8, one launch (start us, length us, event | category | flops | bytes accessed | tf_op | source)
XLA Modules:
  0.0 99.0 jit_solution(1439774186833786830)
XLA Ops:
  0.6 2.5 %pack.1 = bf16[16,272,128]{2,1,0:T(8,128)(2,1)} custom-call(bf16[16,8,896]{2,1,0:T(8,128)(2,1)} %refs_0_.1, bf16[16,8,896]{2,1,0:T(8,128)(2,1)} %refs_1_.1, bf16[16,8,128]{2,1,0:T(8,128)(2,1)} %refs_2_.1, bf16[16,8,128]{2,1,0:T(8,128)(2,1)} %refs_3_.1, bf16[32,128]{1,0:T(8,128)(2,1)} %refs_4_.1, bf16[32,128]{1,0:T(8,128)(2,1)} %refs_5_.1, ...), custom_call_target="tpu_custom_call" | custom-call | tf_op jit(solution)/shard_map/pack/pallas_call | solution.py:366
  3.1 0.0 copy-start
  3.1 0.0 copy-start.1
  3.2 0.0 copy-start.2
  3.2 16.2 %all-to-all-start = ((bf16[16,272,128]{2,1,0:T(8,128)(2,1)}), bf16[16,272,128]{2,1,0:T(8,128)(2,1)S(1)}, u32[]{:S(2)}, u32[]{:S(2)}) async-start(bf16[16,272,128]{2,1,0:T(8,128)(2,1)} %pack.1), calls=%async_computation | async-start | bytes 2228224 | tf_op jit(solution)/shard_map/all_to_all | solution.py:381
  19.4 27.1 %all-to-all-done.recv_ref = bf16[16,272,128]{2,1,0:T(8,128)(2,1)S(1)} async-done(((bf16[16,272,128]{2,1,0:T(8,128)(2,1)}), bf16[16,272,128]{2,1,0:T(8,128)(2,1)S(1)}, u32[]{:S(2)}, u32[]{:S(2)}) %all-to-all-start) | async-done | bytes 1114144 | tf_op jit(solution)/shard_map/all_to_all | solution.py:381
  46.5 0.0 copy-done
  46.5 0.0 copy-done.1
  46.5 0.0 copy-done.2
  46.5 4.4 %stats.1 = (bf16[32,32,128]{2,1,0:T(8,128)(2,1)}, f32[1,896]{1,0:T(1,128)S(1)}, f32[1,896]{1,0:T(1,128)S(1)}) custom-call(s32[8]{0:T(128)S(1)} %copy-done, s32[8]{0:T(128)S(1)} %copy-done.1, s32[2]{0:T(128)S(1)} %copy-done.2, s32[1,896]{1,0:T(1,128)S(1)} %fusion.1.places_ref, bf16[16,272,128]{2,1,0:T(8,128)(2,1)S(1)} %all-to-all-done.recv_ref), custom_call_target="tpu_custom_call" | custom-call | flops 822083584 | bytes 2097152 | tf_op jit(solution)/shard_map/stats/pallas_call | solution.py:395
  50.9 9.4 %all-to-all-start.1 = ((bf16[32,32,128]{2,1,0:T(8,128)(2,1)}), bf16[32,32,128]{2,1,0:T(8,128)(2,1)S(1)}, u32[]{:S(2)}, u32[]{:S(2)}) async-start(bf16[32,32,128]{2,1,0:T(8,128)(2,1)} %get-tuple-element.20), calls=%async_computation.1 | async-start | bytes 524288 | tf_op jit(solution)/shard_map/all_to_all | solution.py:417
  60.2 3.2 %grads.1 = (bf16[768,128]{1,0:T(8,128)(2,1)S(1)}, bf16[768,128]{1,0:T(8,128)(2,1)S(1)}, f32[896,128]{1,0:T(8,128)S(1)}) custom-call(s32[8]{0:T(128)S(1)} %copy-done, s32[8]{0:T(128)S(1)} %copy-done.1, s32[2]{0:T(128)S(1)} %copy-done.2, s32[1,896]{1,0:T(1,128)S(1)} %fusion.1.places_ref, bf16[16,272,128]{2,1,0:T(8,128)(2,1)S(1)} %all-to-all-done.recv_ref, ...), custom_call_target="tpu_custom_call" | custom-call | flops 1468006400 | bytes 16777216 | tf_op jit(solution)/shard_map/grads/pallas_call | solution.py:420
  63.4 4.1 %all-to-all-done.1.sys_ref = bf16[32,32,128]{2,1,0:T(8,128)(2,1)S(1)} async-done(((bf16[32,32,128]{2,1,0:T(8,128)(2,1)}), bf16[32,32,128]{2,1,0:T(8,128)(2,1)S(1)}, u32[]{:S(2)}, u32[]{:S(2)}) %all-to-all-start.1) | async-done | bytes 262176 | tf_op jit(solution)/shard_map/all_to_all | solution.py:417
  67.6 0.9 gather.1
  68.5 11.3 %all-to-all-start.2 = ((bf16[16,160,128]{2,1,0:T(8,128)(2,1)}), bf16[16,160,128]{2,1,0:T(8,128)(2,1)S(1)}, u32[]{:S(2)}, u32[]{:S(2)}) async-start(bf16[16,160,128]{2,1,0:T(8,128)(2,1)} %gather.1), calls=%async_computation.2 | async-start | bytes 1310720 | tf_op jit(solution)/shard_map/all_to_all | solution.py:449
  79.8 0.2 fusion.swap_ref
  80.0 17.4 %all-to-all-done.2.recv_ref = bf16[16,160,128]{2,1,0:T(8,128)(2,1)S(1)} async-done(((bf16[16,160,128]{2,1,0:T(8,128)(2,1)}), bf16[16,160,128]{2,1,0:T(8,128)(2,1)S(1)}, u32[]{:S(2)}, u32[]{:S(2)}) %all-to-all-start.2) | async-done | bytes 655392 | tf_op jit(solution)/shard_map/all_to_all | solution.py:449
  97.4 1.6 %finish.1 = (f32[16,8,896]{2,1,0:T(8,128)}, f32[2,32,128]{2,1,0:T(8,128)}, f32[2,32,128]{2,1,0:T(8,128)}, f32[16,8,128]{2,1,0:T(8,128)}, f32[16,8,128]{2,1,0:T(8...) custom-call(s32[8]{0:T(128)S(1)} %copy-done, bf16[128,128]{1,0:T(8,128)(2,1)S(1)} %fusion.swap_ref, ...), custom_call_target="tpu_custom_call" | custom-call | tf_op jit(solution)/shard_map/finish/pallas_call | solution.py:461
  (4 shorter events, 0.0 us)
Async XLA Ops:
  3.1 43.3 %copy-start = (s32[8]{0:T(128)S(1)}, s32[8]{0:T(128)}, u32[]{:S(2)}) copy-start(s32[8]{0:T(128)} %parent_ref.5) | copy-start | bytes 100
  3.1 43.3 %copy-start.1 = (s32[8]{0:T(128)S(1)}, s32[8]{0:T(128)}, u32[]{:S(2)}) copy-start(s32[8]{0:T(128)} %resp_len_ref.3) | copy-start | bytes 100
  3.2 43.3 %copy-start.2 = (s32[2]{0:T(128)S(1)}, s32[2]{0:T(128)}, u32[]{:S(2)}) copy-start(s32[2]{0:T(128)} %ctx_len_ref.3) | copy-start | bytes 28
  3.2 43.3 %all-to-all-start = ((bf16[16,272,128]{2,1,0:T(8,128)(2,1)}), bf16[16,272,128]{2,1,0:T(8,128)(2,1)S(1)}, u32[]{:S(2)}, u32[]{:S(2)}) async-start(bf16[16,272,128]{2,1,0:T(8,128)(2,1)} %pack.1), calls=%async_computation | async-start | bytes 2228224 | tf_op jit(solution)/shard_map/all_to_all | solution.py:381
  50.9 16.7 %all-to-all-start.1 = ((bf16[32,32,128]{2,1,0:T(8,128)(2,1)}), bf16[32,32,128]{2,1,0:T(8,128)(2,1)S(1)}, u32[]{:S(2)}, u32[]{:S(2)}) async-start(bf16[32,32,128]{2,1,0:T(8,128)(2,1)} %get-tuple-element.20), calls=%async_computation.1 | async-start | bytes 524288 | tf_op jit(solution)/shard_map/all_to_all | solution.py:417
  68.5 28.9 %all-to-all-start.2 = ((bf16[16,160,128]{2,1,0:T(8,128)(2,1)}), bf16[16,160,128]{2,1,0:T(8,128)(2,1)S(1)}, u32[]{:S(2)}, u32[]{:S(2)}) async-start(bf16[16,160,128]{2,1,0:T(8,128)(2,1)} %gather.1), calls=%async_computation.2 | async-start | bytes 1310720 | tf_op jit(solution)/shard_map/all_to_all | solution.py:449

commit v5 on v4

--- a/solution.py
+++ b/solution.py
@@ -29,7 +29,7 @@
 NEGATIVE = -1e30
 FIRST_IN = 8
 FIRST_SYS = 21
-FIRST_OUT = 8
+FIRST_OUT = 12
 BLOCK = 256
 CHUNK = 64
 RATE = SCALING * math.log2(math.e)

time: 99.3 us -> 99.4 us (level)
  the two profiles are of different devices: /device:TPU:8 before, /device:TPU:1 now
where the time goes in v5:
time: 99.4 us; the launch traced here: 99 us
  waiting for transfers between devices  44.6 us (45%)
  starting transfers between devices  40.9 us (41%)
  Pallas kernels  12.6 us (13%)
    all_to_all x1, waiting for transfers between devices, shards(): lax.all_to_all(send, 'level', 0, 0, axis_index_groups=[order(FIRST_IN, LE...  25.4 us
    all_to_all x1, starting transfers between devices, shards(): lax.all_to_all(send, 'level', 0, 0, axis_index_groups=[order(FIRST_IN, LE...  16.5 us
    all_to_all x1, waiting for transfers between devices, shards(): lax.all_to_all(send, 'level', 0, 0, axis_index_groups=[order(FIRST_OUT, L...  15.6 us
    all_to_all x1, starting transfers between devices, shards(): lax.all_to_all(send, 'level', 0, 0, axis_index_groups=[order(FIRST_OUT, L...  13.6 us
    all_to_all x1, starting transfers between devices, shards(): lax.all_to_all(sys_send, 'req', 0, 0, axis_index_groups=[order(FIRST_SYS,...  10.7 us
    pallas_call x1, Pallas kernels, shards(): pl.pallas_call(stats_kernel, out_shape=[shape((SYS_ROWS, 2 * LEVELS, HEAD...  4.38 us
    all_to_all x1, waiting for transfers between devices, shards(): lax.all_to_all(sys_send, 'req', 0, 0, axis_index_groups=[order(FIRST_SYS,...  3.58 us
    pallas_call x1, Pallas kernels, shards(): pl.pallas_call(grads_kernel, out_shape=[shape((CTX + CH, HEAD_DIM), bf16)...  3.21 us
  transfers between devices with their start and end apart: 3, of which 3 were waited for; matrix products, arithmetic and copies ran while one was open for 0% of the time, Pallas kernels for 3%

profile of v5, /device:TPU:1, one launch (start us, length us, event | category | flops | bytes accessed | tf_op | source)
XLA Modules:
  0.0 99.0 jit_solution(17738386982600973590)
XLA Ops:
  0.6 2.5 %pack.1 = bf16[16,272,128]{2,1,0:T(8,128)(2,1)} custom-call(bf16[16,8,896]{2,1,0:T(8,128)(2,1)} %refs_0_.1, bf16[16,8,896]{2,1,0:T(8,128)(2,1)} %refs_1_.1, bf16[16,8,128]{2,1,0:T(8,128)(2,1)} %refs_2_.1, bf16[16,8,128]{2,1,0:T(8,128)(2,1)} %refs_3_.1, bf16[32,128]{1,0:T(8,128)(2,1)} %refs_4_.1, bf16[32,128]{1,0:T(8,128)(2,1)} %refs_5_.1, ...), custom_call_target="tpu_custom_call" | custom-call | tf_op jit(solution)/shard_map/pack/pallas_call | solution.py:366
  3.1 0.0 copy-start
  3.2 0.0 copy-start.1
  3.2 0.0 copy-start.2
  3.2 16.5 %all-to-all-start = ((bf16[16,272,128]{2,1,0:T(8,128)(2,1)}), bf16[16,272,128]{2,1,0:T(8,128)(2,1)S(1)}, u32[]{:S(2)}, u32[]{:S(2)}) async-start(bf16[16,272,128]{2,1,0:T(8,128)(2,1)} %pack.1), calls=%async_computation | async-start | bytes 2228224 | tf_op jit(solution)/shard_map/all_to_all | solution.py:381
  19.7 25.4 %all-to-all-done.recv_ref = bf16[16,272,128]{2,1,0:T(8,128)(2,1)S(1)} async-done(((bf16[16,272,128]{2,1,0:T(8,128)(2,1)}), bf16[16,272,128]{2,1,0:T(8,128)(2,1)S(1)}, u32[]{:S(2)}, u32[]{:S(2)}) %all-to-all-start) | async-done | bytes 1114144 | tf_op jit(solution)/shard_map/all_to_all | solution.py:381
  45.1 0.0 copy-done
  45.1 0.0 copy-done.1
  45.1 0.0 copy-done.2
  45.1 4.4 %stats.1 = (bf16[32,32,128]{2,1,0:T(8,128)(2,1)}, f32[1,896]{1,0:T(1,128)S(1)}, f32[1,896]{1,0:T(1,128)S(1)}) custom-call(s32[8]{0:T(128)S(1)} %copy-done, s32[8]{0:T(128)S(1)} %copy-done.1, s32[2]{0:T(128)S(1)} %copy-done.2, s32[1,896]{1,0:T(1,128)S(1)} %fusion.1.places_ref, bf16[16,272,128]{2,1,0:T(8,128)(2,1)S(1)} %all-to-all-done.recv_ref), custom_call_target="tpu_custom_call" | custom-call | flops 822083584 | bytes 2097152 | tf_op jit(solution)/shard_map/stats/pallas_call | solution.py:395
  49.5 10.7 %all-to-all-start.1 = ((bf16[32,32,128]{2,1,0:T(8,128)(2,1)}), bf16[32,32,128]{2,1,0:T(8,128)(2,1)S(1)}, u32[]{:S(2)}, u32[]{:S(2)}) async-start(bf16[32,32,128]{2,1,0:T(8,128)(2,1)} %get-tuple-element.20), calls=%async_computation.1 | async-start | bytes 524288 | tf_op jit(solution)/shard_map/all_to_all | solution.py:417
  60.2 3.2 %grads.1 = (bf16[768,128]{1,0:T(8,128)(2,1)S(1)}, bf16[768,128]{1,0:T(8,128)(2,1)S(1)}, f32[896,128]{1,0:T(8,128)S(1)}) custom-call(s32[8]{0:T(128)S(1)} %copy-done, s32[8]{0:T(128)S(1)} %copy-done.1, s32[2]{0:T(128)S(1)} %copy-done.2, s32[1,896]{1,0:T(1,128)S(1)} %fusion.1.places_ref, bf16[16,272,128]{2,1,0:T(8,128)(2,1)S(1)} %all-to-all-done.recv_ref, ...), custom_call_target="tpu_custom_call" | custom-call | flops 1468006400 | bytes 16777216 | tf_op jit(solution)/shard_map/grads/pallas_call | solution.py:420
  63.4 3.6 %all-to-all-done.1.sys_ref = bf16[32,32,128]{2,1,0:T(8,128)(2,1)S(1)} async-done(((bf16[32,32,128]{2,1,0:T(8,128)(2,1)}), bf16[32,32,128]{2,1,0:T(8,128)(2,1)S(1)}, u32[]{:S(2)}, u32[]{:S(2)}) %all-to-all-start.1) | async-done | bytes 262176 | tf_op jit(solution)/shard_map/all_to_all | solution.py:417
  67.0 0.9 gather.1
  67.9 13.6 %all-to-all-start.2 = ((bf16[16,160,128]{2,1,0:T(8,128)(2,1)}), bf16[16,160,128]{2,1,0:T(8,128)(2,1)S(1)}, u32[]{:S(2)}, u32[]{:S(2)}) async-start(bf16[16,160,128]{2,1,0:T(8,128)(2,1)} %gather.1), calls=%async_computation.2 | async-start | bytes 1310720 | tf_op jit(solution)/shard_map/all_to_all | solution.py:449
  81.6 0.2 fusion.swap_ref
  81.8 15.6 %all-to-all-done.2.recv_ref = bf16[16,160,128]{2,1,0:T(8,128)(2,1)S(1)} async-done(((bf16[16,160,128]{2,1,0:T(8,128)(2,1)}), bf16[16,160,128]{2,1,0:T(8,128)(2,1)S(1)}, u32[]{:S(2)}, u32[]{:S(2)}) %all-to-all-start.2) | async-done | bytes 655392 | tf_op jit(solution)/shard_map/all_to_all | solution.py:449
  97.4 1.6 %finish.1 = (f32[16,8,896]{2,1,0:T(8,128)}, f32[2,32,128]{2,1,0:T(8,128)}, f32[2,32,128]{2,1,0:T(8,128)}, f32[16,8,128]{2,1,0:T(8,128)}, f32[16,8,128]{2,1,0:T(8...) custom-call(s32[8]{0:T(128)S(1)} %copy-done, bf16[128,128]{1,0:T(8,128)(2,1)S(1)} %fusion.swap_ref, ...), custom_call_target="tpu_custom_call" | custom-call | tf_op jit(solution)/shard_map/finish/pallas_call | solution.py:461
  (4 shorter events, 0.0 us)
Async XLA Ops:
  3.1 41.9 %copy-start = (s32[8]{0:T(128)S(1)}, s32[8]{0:T(128)}, u32[]{:S(2)}) copy-start(s32[8]{0:T(128)} %parent_ref.5) | copy-start | bytes 100
  3.2 41.9 %copy-start.1 = (s32[8]{0:T(128)S(1)}, s32[8]{0:T(128)}, u32[]{:S(2)}) copy-start(s32[8]{0:T(128)} %resp_len_ref.3) | copy-start | bytes 100
  3.2 41.9 %copy-start.2 = (s32[2]{0:T(128)S(1)}, s32[2]{0:T(128)}, u32[]{:S(2)}) copy-start(s32[2]{0:T(128)} %ctx_len_ref.3) | copy-start | bytes 28
  3.2 41.9 %all-to-all-start = ((bf16[16,272,128]{2,1,0:T(8,128)(2,1)}), bf16[16,272,128]{2,1,0:T(8,128)(2,1)S(1)}, u32[]{:S(2)}, u32[]{:S(2)}) async-start(bf16[16,272,128]{2,1,0:T(8,128)(2,1)} %pack.1), calls=%async_computation | async-start | bytes 2228224 | tf_op jit(solution)/shard_map/all_to_all | solution.py:381
  49.5 17.5 %all-to-all-start.1 = ((bf16[32,32,128]{2,1,0:T(8,128)(2,1)}), bf16[32,32,128]{2,1,0:T(8,128)(2,1)S(1)}, u32[]{:S(2)}, u32[]{:S(2)}) async-start(bf16[32,32,128]{2,1,0:T(8,128)(2,1)} %get-tuple-element.20), calls=%async_computation.1 | async-start | bytes 524288 | tf_op jit(solution)/shard_map/all_to_all | solution.py:417
  67.9 29.5 %all-to-all-start.2 = ((bf16[16,160,128]{2,1,0:T(8,128)(2,1)}), bf16[16,160,128]{2,1,0:T(8,128)(2,1)S(1)}, u32[]{:S(2)}, u32[]{:S(2)}) async-start(bf16[16,160,128]{2,1,0:T(8,128)(2,1)} %gather.1), calls=%async_computation.2 | async-start | bytes 1310720 | tf_op jit(solution)/shard_map/all_to_all | solution.py:449
